TPU v7x, 768 devices: a whole 4x8x12 slice. The times are simulated.
768 devices in a mesh: blk: 32 (over y, x), rep: 24 (over z, core).
Axes of the slice: x: 4, y: 8, z: 12, core: 2. Of those that a mesh axis runs over, the one named last changes fastest.
Arguments:
- features: bfloat16 [393216, 256], P(('blk', 'rep')), may hold values from -6 to 6
- weight: bfloat16 [256, 256], replicated, may hold values from -1.5 to 1.5
- cotangent: bfloat16 [393216, 256], P(('blk', 'rep')), may hold values from -6 to 6
- edge_source: int32 [393216, 16], P(('blk', 'rep')), may hold values from 0 to 3583
- edge_mult: int32 [393216, 16], P(('blk', 'rep')), may hold values from 1 to 4
- read_blocks: int32 [768, 32, 1], P(('blk', 'rep')), may hold values from 0 to 7, as said below
- hub_blocks: int32 [16], replicated, may hold values from 0 to 6143, as said below
Outputs:
- output: bfloat16 [393216, 256], P(('blk', 'rep'))
- feature_grad: float32 [393216, 256], P(('blk', 'rep'))
- weight_grad: float32 [256, 256], replicated
Inputs may be any that keep to these rules, and one draw needn't show every extreme that they name: `read_blocks`: for each device and peer the 1 entries are distinct local block indices of that peer. `hub_blocks`: the 16 ids are distinct; block 0 and block 6143 are always among them.
All inputs are finite; a program needn't handle non-finite values.
Results may differ from a plain program's by a relative error of at most 0.015.
Values may be sent and summed in bfloat16 or wider, within the bound.
No kernel may reach another device: no remote copies, remote signals or barrier semaphores. Data moves between devices by JAX's collectives and lax.ppermute only.
A program may use at most 32 MiB of HBM per device.

v0:
```python
import jax
import jax.numpy as jnp
from jax import lax
from jax.sharding import PartitionSpec as P

BR = 64


def silu_slope(value):
    sig = jax.nn.sigmoid(value)
    return sig * (1.0 + value * (1.0 - sig))


def shards(features, weight, cotangent, edge_source, edge_mult, read_blocks, hub_blocks):
    per_dev, width = features.shape
    blocks_dev = per_dev // BR
    hubs = hub_blocks.shape[0]
    device = lax.axis_index(("blk", "rep"))
    own_blocks = features.reshape(blocks_dev, BR, width)
    hub_owner = hub_blocks // blocks_dev
    hub_local = hub_blocks % blocks_dev
    picked = own_blocks[hub_local].astype(jnp.float32)
    mine = hub_owner == device
    offered = jnp.where(mine[:, None, None], picked, 0.0)
    hub_rows = lax.psum(offered, ("blk", "rep")).astype(jnp.bfloat16)
    wanted = read_blocks[0]
    requested = lax.all_to_all(wanted, "blk", split_axis=0, concat_axis=0, tiled=True)
    outgoing = own_blocks[requested]
    incoming = lax.all_to_all(outgoing, "blk", split_axis=0, concat_axis=0, tiled=True)
    table = jnp.concatenate(
        [features, hub_rows.reshape(-1, width), incoming.reshape(-1, width)], axis=0
    )
    mult = edge_mult.astype(jnp.float32)
    edge_weight = mult / jnp.sum(mult, axis=1, keepdims=True)
    rows = table[edge_source]
    aggregated = jnp.einsum(
        "nk,nkf->nf", edge_weight, rows, preferred_element_type=jnp.float32
    ).astype(jnp.bfloat16)
    pre = jnp.dot(aggregated, weight, preferred_element_type=jnp.float32)
    output = jax.nn.silu(pre).astype(jnp.bfloat16)
    pre_grad = (cotangent.astype(jnp.float32) * silu_slope(pre)).astype(jnp.bfloat16)
    local_wgrad = lax.dot_general(
        aggregated, pre_grad, (((0,), (0,)), ((), ())), preferred_element_type=jnp.float32
    )
    agg_grad = lax.dot_general(
        pre_grad, weight, (((1,), (1,)), ((), ())), preferred_element_type=jnp.float32
    ).astype(jnp.bfloat16)
    terms = edge_weight[:, :, None] * agg_grad.astype(jnp.float32)[:, None, :]
    table_grad = jax.ops.segment_sum(
        terms.reshape(-1, width), edge_source.reshape(-1), num_segments=table.shape[0]
    )
    hub_start = per_dev + hubs * BR
    local_grad = table_grad[:per_dev]
    hub_grad = table_grad[per_dev:hub_start].reshape(hubs, BR, width)
    remote_grad = table_grad[hub_start:].reshape(incoming.shape).astype(jnp.bfloat16)
    returned = lax.all_to_all(remote_grad, "blk", split_axis=0, concat_axis=0, tiled=True)
    hub_total, weight_grad = lax.psum((hub_grad, local_wgrad), ("blk", "rep"))
    block_ids = jnp.arange(blocks_dev, dtype=jnp.int32)
    hub_pick = ((hub_owner == device)[:, None] & (hub_local[:, None] == block_ids[None, :])).astype(
        jnp.float32
    )
    own_hub = jnp.einsum("hb,hrf->brf", hub_pick, hub_total, precision=lax.Precision.HIGHEST)
    request_pick = (requested[:, :, None] == block_ids[None, None, :]).astype(jnp.bfloat16)
    own_remote = jnp.einsum(
        "psb,psrf->brf", request_pick, returned, preferred_element_type=jnp.float32
    )
    feature_grad = local_grad + (own_hub + own_remote).reshape(per_dev, width)
    return (output, feature_grad, weight_grad)


def solution(mesh):
    in_specs = (
        P(("blk", "rep"), None),
        P(),
        P(("blk", "rep"), None),
        P(("blk", "rep"), None),
        P(("blk", "rep"), None),
        P(("blk", "rep"), None, None),
        P(),
    )
    out_specs = (P(("blk", "rep"), None), P(("blk", "rep"), None), P())
    return jax.shard_map(shards, mesh=mesh, in_specs=in_specs, out_specs=out_specs, check_vma=False)
```

profile of v0, /device:TPU:1, one launch (start us, length us, event | category | flops | bytes accessed | tf_op | source)
XLA Modules:
  0.0 772.3 jit_solution(7123314729805328211)
XLA Ops:
  7.2 0.0 copy-start
  7.2 0.0 copy-start.1
  7.2 0.0 copy-start.5
  7.2 0.0 copy-start.3
  7.2 0.0 copy-start.7
  7.2 0.8 copy.24
  8.0 18.9 %all_to_all.22 = s32[32,1,1]{2,1,0:T(1,128)S(1)} all-to-all(s32[32,1,1]{2,1,0:T(1,128)S(1)} %copy.24), channel_id=1, replica_groups=mesh['blk'=32,'rep'=24] {'blk'}, dimensions={0} | all-to-all | bytes 256 | tf_op jit(solution)/shard_map/all_to_all | solution.py:27
  26.9 1.2 fusion.18
  28.1 2.5 gather_fusion.1
  30.7 3.9 all-to-all-start.1
  34.6 0.0 copy-done.5
  34.6 0.1 copy.26
  34.8 0.1 copy.25
  34.9 0.1 reshape.135
  35.0 0.0 copy-done.3
  35.1 0.1 copy.27
  35.2 0.1 mul.36
  35.4 0.9 copy.32
  36.3 0.1 reshape.143
  36.4 0.0 copy-done.7
  36.5 0.0 copy-done.1
  36.5 0.6 gather_fusion
  37.1 0.1 convert_select_fusion
  37.3 137.6 %all-reduce.5 = bf16[16,64,256]{2,1,0:T(8,128)(2,1)} all-reduce(f32[16,64,256]{2,1,0:T(8,128)S(1)} %convert_select_fusion), channel_id=1, replica_groups=mesh['blk'=32,'rep'=24] {'blk','rep'}, use_global_device_ids=true, to_apply=%region_1.2 | all-reduce | flops 262144 | bytes 1572864 | tf_op jit(solution)/shard_map/psum | solution.py:25
  174.8 0.0 all-to-all-done.1
  174.8 1.2 pad_maximum_fusion
  176.0 0.0 copy-start.2
  176.0 33.1 %gather_fusion.2 = bf16[8192,256]{1,0:T(8,128)(2,1)} fusion(bf16[3584,256]{1,0:T(8,128)(2,1)S(1)} %pad_maximum_fusion, s32[8192]{0:T(1024)S(1)} %broadcast_clamp_fusion), kind=kCustom, calls=%fused_computation.2 | custom fusion | bytes 8421376 | tf_op jit(solution)/shard_map/gather | solution.py:35
  209.1 0.0 copy-done.2
  209.1 2.9 fusion.19
  212.0 1.1 multiply_convert_fusion
  213.1 0.2 fusion.2
  213.4 3.8 bitcast_multiply_fusion
  217.2 46.6 %scatter_custom_fusion = f32[3584,256]{1,0:T(8,128)} fusion(s32[8192]{0:T(1024)S(1)} %reshape.143, f32[8192,256]{1,0:T(8,128)} %bitcast_multiply_fusion, f32[]{:T(128)} %constant.20.clone.1), kind=kCustom, calls=%fused_computation.7 | custom fusion | flops 2097152 | bytes 3670528 | tf_op jit(solution)/shard_map/scatter-add | solution.py:49
  263.8 2.7 slice.24
  266.6 10.8 %all-to-all-start.2 = ((bf16[32,1,64,256]{3,2,1,0:T(8,128)(2,1)}), bf16[32,1,64,256]{3,2,1,0:T(8,128)(2,1)S(1)}, u32[]{:S(2)}, u32[]{:S(2)}) async-start(bf16[32,1,64,256]{3,2,1,0:T(8,128)(2,1)} %bitcast.14), calls=%async_computation.2 | async-start | bytes 2097152 | tf_op jit(solution)/shard_map/all_to_all | solution.py:56
  277.4 0.0 all-reduce.4.cloned.1.call-start
  277.5 0.0 slice-done
  277.5 1.6 copy.28
  279.1 1.0 fusion.5
  280.1 0.0 all-reduce.4.cloned.1.call-update
  280.1 480.2 %all-reduce.4.cloned.1.call-done = (f32[16,64,256]{2,0,1:T(8,128)}, f32[256,256]{1,0:T(8,128)}) async-done(((f32[16,64,256]{2,0,1:T(8,128)}, f32[256,256]{1,0:T(8,128)}), (f32[16,64,256]{2,0,1:T(8,128)}, f32[256,256]{1,0:T(8,128)})) %all-reduce.4.cloned.1.call-update) | async-done | bytes 1310736 | tf_op jit(solution)/shard_map/psum | solution.py:57
  760.3 1.7 fusion.10
  762.0 0.0 all-to-all-done.2
  762.0 0.7 convolution_add_fusion
  762.7 0.2 copy.31
  762.9 1.9 slice_add_fusion
  764.8 0.7 copy.47
  (15 shorter events, 0.1 us)
Async XLA Ops:
  7.2 204.8 %copy-start = (bf16[256,256]{1,0:T(8,128)(2,1)S(1)}, bf16[256,256]{1,0:T(8,128)(2,1)}, u32[]{:S(2)}) copy-start(bf16[256,256]{1,0:T(8,128)(2,1)} %param.8) | copy-start | bytes 393220
  7.2 29.3 %copy-start.1 = (bf16[512,256]{1,0:T(8,128)(2,1)S(1)}, bf16[512,256]{1,0:T(8,128)(2,1)}, u32[]{:S(2)}) copy-start(bf16[512,256]{1,0:T(8,128)(2,1)} %param.7) | copy-start | bytes 786436
  7.2 27.4 %copy-start.5 = (s32[512,16]{0,1:T(8,128)S(1)}, s32[512,16]{0,1:T(8,128)}, u32[]{:S(2)}) copy-start(s32[512,16]{0,1:T(8,128)} %param.10) | copy-start | bytes 98308
  7.2 27.8 %copy-start.3 = (s32[512,16]{0,1:T(8,128)S(1)}, s32[512,16]{0,1:T(8,128)}, u32[]{:S(2)}) copy-start(s32[512,16]{0,1:T(8,128)} %param.11) | copy-start | bytes 98308
  7.2 29.2 %copy-start.7 = (s32[16]{0:T(128)S(1)}, s32[16]{0:T(128)}, u32[]{:S(2)}) copy-start(s32[16]{0:T(128)} %param.13) | copy-start | bytes 196
  30.7 144.2 %all-to-all-start.1 = ((bf16[32,1,64,256]{3,2,1,0:T(8,128)(2,1)}), bf16[32,1,64,256]{3,2,1,0:T(8,128)(2,1)S(1)}, u32[]{:S(2)}, u32[]{:S(2)}) async-start(bf16[32,1,64,256]{3,2,1,0:T(8,128)(2,1)} %bitcast.4), calls=%async_computation.1 | async-start | bytes 2097152 | tf_op jit(solution)/shard_map/all_to_all | solution.py:29
  176.0 33.1 %copy-start.2 = (bf16[512,16,1]{1,2,0:T(2,128)(2,1)S(1)}, bf16[512,16,1]{1,2,0:T(2,128)(2,1)}, u32[]{:S(2)}) copy-start(bf16[512,16,1]{1,2,0:T(2,128)(2,1)} %copy.32) | copy-start | bytes 49156
  209.1 3.0 copy-start.6
  263.8 13.6 %slice-start = ((f32[3584,256]{1,0:T(8,128)}), f32[1024,256]{1,0:T(8,128)S(1)}, s32[]{:S(2)}) async-start(f32[3584,256]{1,0:T(8,128)} %scatter_custom_fusion), calls=%async_computation.4 | async-start | bytes 2097152 | tf_op jit(solution)/shard_map/slice | solution.py:54
  266.6 495.4 %all-to-all-start.2 = ((bf16[32,1,64,256]{3,2,1,0:T(8,128)(2,1)}), bf16[32,1,64,256]{3,2,1,0:T(8,128)(2,1)S(1)}, u32[]{:S(2)}, u32[]{:S(2)}) async-start(bf16[32,1,64,256]{3,2,1,0:T(8,128)(2,1)} %bitcast.14), calls=%async_computation.2 | async-start | bytes 2097152 | tf_op jit(solution)/shard_map/all_to_all | solution.py:56
  277.4 482.9 %all-reduce.4.cloned.1.call-start = ((), (), s32[]{:S(2)}) async-start(), calls=%async_computation.3 | async-start | bytes 2621440 | tf_op jit(solution)/shard_map/psum | solution.py:57
  760.3 4.5 copy-start.4
Sparse Core Ops, SparseCore 0:
  284.5 475.7 all-reduce.3
where the time goes:
time: 773 us; the launch traced here: 772 us
  waiting for transfers between devices  480 us (62%)
  blocking collectives  156 us (20%)
  other arithmetic  55 us (7%)
  local copies, waits for them, and re-layouts  43.9 us (6%)
  starting transfers between devices  14.8 us (2%)
  between operations  14.3 us (2%)
    psum x1, waiting for transfers between devices, shards(): hub_total, weight_grad = lax.psum((hub_grad, local_wgrad), ('blk', 'rep'))  480 us
    psum x1, blocking collectives, shards(): hub_rows = lax.psum(offered, ('blk', 'rep')).astype(jnp.bfloat16)  138 us
    scatter-add x1, other arithmetic, shards(): jax.ops.segment_sum(terms.reshape(-1, width), edge_source.reshape(-1), nu...  46.6 us
    gather x1, local copies, waits for them, and re-layouts, shards(): rows = table[edge_source]  33.1 us
    all_to_all x1, blocking collectives, shards(): lax.all_to_all(wanted, 'blk', split_axis=0, concat_axis=0, tiled=True)  18.9 us
  transfers between devices with their start and end apart: 3, of which 1 were waited for; matrix products, arithmetic and copies ran while one was open for 1% of the time, Pallas kernels for 0%

commit v1 on v0

v1 whole, which is shorter than its diff:
```python
import functools

import jax
import jax.numpy as jnp
from jax import lax
from jax.experimental import pallas as pl
from jax.experimental.pallas import tpu as pltpu
from jax.sharding import Mesh, PartitionSpec as P

BR = 64
HALF = BR // 2
GROUP = 16
CHUNK = 24
BF = jnp.bfloat16
F32 = jnp.float32
NT = (((1,), (1,)), ((), ()))
TN = (((0,), (0,)), ((), ()))
VMEM = pl.BlockSpec(memory_space=pltpu.VMEM)
SMEM = pl.BlockSpec(memory_space=pltpu.SMEM)
ANY = pl.BlockSpec(memory_space=pl.ANY)


def call(body, out, in_specs, scratch=(), flops=0, traffic=1 << 20, limit=8, aliases=None):
    several = isinstance(out, (list, tuple))
    return pl.pallas_call(
        body,
        out_shape=out,
        in_specs=in_specs,
        out_specs=[VMEM] * len(out) if several else VMEM,
        scratch_shapes=list(scratch),
        input_output_aliases=aliases or {},
        compiler_params=pltpu.CompilerParams(vmem_limit_bytes=limit << 20),
        cost_estimate=pl.CostEstimate(flops=flops, bytes_accessed=traffic, transcendentals=0),
    )


def build_body(idx_ref, mult_ref, _, m_ref, mt_ref, inv_ref):
    groups, _, lanes = idx_ref.shape
    cols = m_ref.shape[2] // 128
    own = (lax.broadcasted_iota(jnp.int32, (GROUP, lanes), 1) // 16) == lax.broadcasted_iota(
        jnp.int32, (GROUP, lanes), 0
    )
    low = lax.broadcasted_iota(jnp.int32, (128, lanes), 0)

    def group(g, carry):
        idx = idx_ref[g]
        high = idx >> 7
        onehot = jnp.where(low == (idx & 127), 1.0, 0.0).astype(BF)
        mult = jnp.where(own, mult_ref[g].astype(F32), 0.0)
        inv_ref[g] = jnp.broadcast_to(1.0 / jnp.sum(mult, axis=1, keepdims=True), (GROUP, 128))
        left = jnp.concatenate([jnp.where(high == k, mult, 0.0).astype(BF) for k in range(cols)], axis=0)
        dense = lax.dot_general(left, onehot, NT, preferred_element_type=F32).astype(BF)
        for k in range(cols):
            m_ref[g, :, k * 128 : (k + 1) * 128] = dense[k * GROUP : (k + 1) * GROUP]
        return carry

    lax.fori_loop(0, groups, group, 0)
    per = 128 // GROUP

    def turn(k, carry):
        rows = pl.ds(pl.multiple_of(k * 128, 128), 128)
        for n in range(groups // per):
            tile = m_ref[n * per : (n + 1) * per, :, rows].reshape(128, 128)
            mt_ref[rows, n * 128 : (n + 1) * 128] = tile.T
        return carry

    lax.fori_loop(0, cols, turn, 0)


def offer_body(which_ref, wanted_ref, kept_ref, got_ref, out_ref, token_ref):
    rows = kept_ref.shape[0]
    for h in range(out_ref.shape[0] // 2):
        at = which_ref[h]
        inner = jnp.where(at < rows, at, at - rows)
        block = jnp.where(at < rows, kept_ref[inner], got_ref[inner])
        for j in range(2):
            p = 2 * h + j
            out_ref[p, 0:16, :] = block[j * 16 : j * 16 + 16]
            out_ref[p, 16:24, :] = jnp.full((8, out_ref.shape[2]), wanted_ref[p].astype(F32), F32).astype(BF)
    token_ref[...] = jnp.zeros_like(token_ref)


def spread_body(which_ref, source_ref, _, out_ref):
    chosen = source_ref[which_ref[0], 0:16, :]
    for i in range(out_ref.shape[0]):
        out_ref[i] = chosen


def serve_body(which_ref, hub_ref, blocks_ref, pieces_ref, out_ref):
    piece = pieces_ref[hub_ref[0]]
    for i in range(out_ref.shape[0]):
        out_ref[i, 0:BR, :] = blocks_ref[which_ref[i]]
        out_ref[i, BR : BR + 16, :] = piece


def first_body(m_ref, feat_ref, in_ref, acc_ref):
    step = 128
    per_dev, width = feat_ref.shape
    n_half = in_ref.shape[0] * 16
    blocks = in_ref[:, 0:BR, :].reshape(-1, width)
    hubs = in_ref[:, BR : BR + 16, :].reshape(-1, width)

    def rows_of(i, carry):
        rows = pl.ds(pl.multiple_of(i * step, step), step)
        total = jnp.dot(m_ref[rows, 0:per_dev], feat_ref[...], preferred_element_type=F32)
        total += jnp.dot(m_ref[rows, per_dev : per_dev + n_half], hubs, preferred_element_type=F32)
        total += jnp.dot(m_ref[rows, per_dev + 2 * n_half :], blocks, preferred_element_type=F32)
        acc_ref[rows, :] = total
        return carry

    lax.fori_loop(0, per_dev // step, rows_of, 0)


def layer_body(core_ref, acc_ref, m_ref, mt_ref, inv_ref, hub_ref, weight_ref, cot_ref,
               out_ref, gs_ref, keep_ref, send_ref, agg_s, pg_s, w_s):
    step = 128
    per_dev, width = acc_ref.shape
    n_half = hub_ref.shape[0]

    def rows_of(i, carry):
        rows = pl.ds(pl.multiple_of(i * step, step), step)
        total = acc_ref[rows, :] + jnp.dot(
            m_ref[rows, per_dev + n_half : per_dev + 2 * n_half], hub_ref[...], preferred_element_type=F32
        )
        inv = inv_ref[rows, :]
        inv = jnp.concatenate([inv] * (width // 128), axis=1)
        agg = (total * inv).astype(BF)
        agg_s[rows, :] = agg
        pre = jnp.dot(agg, weight_ref[...], preferred_element_type=F32)
        sig = jax.nn.sigmoid(pre)
        out_ref[rows, :] = (pre * sig).astype(BF)
        slope = sig * (1.0 + pre * (1.0 - sig))
        pg = (cot_ref[rows, :].astype(F32) * slope).astype(BF)
        pg_s[rows, :] = pg
        ag = lax.dot_general(pg, weight_ref[...], NT, preferred_element_type=F32).astype(BF)
        gs_ref[rows, :] = (ag.astype(F32) * inv).astype(BF)
        return carry

    lax.fori_loop(0, per_dev // step, rows_of, 0)
    grads = gs_ref[...]
    w_s[...] = lax.dot_general(agg_s[...], pg_s[...], TN, preferred_element_type=F32)
    half = width // 2
    core = core_ref[0]
    for ref, base, part in ((send_ref, per_dev + n_half, 1 - core), (keep_ref, per_dev, core)):
        for k in range(n_half // 256):
            rows = mt_ref[base + k * 256 : base + (k + 1) * 256, :]
            piece = jnp.dot(rows, grads, preferred_element_type=F32).astype(BF)
            ref[k * 16 : (k + 1) * 16, 0:16, :] = piece.reshape(16, 16, width)
        wide = w_s[pl.ds(pl.multiple_of(part * half, half), half), :]
        for d in range(ref.shape[0]):
            tile = wide[(d // 2) * 8 : (d // 2) * 8 + 8, (d % 2) * 128 : (d % 2) * 128 + 128]
            ref[d, 16:24, :] = split(tile)


def table_body(mt_ref, gs_ref, keep_ref, got_ref, local_ref, out_ref):
    grads = gs_ref[...]
    per_dev, width = local_ref.shape
    for k in range(per_dev // 256):
        rows = mt_ref[k * 256 : (k + 1) * 256, :]
        local_ref[k * 256 : (k + 1) * 256, :] = jnp.dot(rows, grads, preferred_element_type=F32)
    peers = out_ref.shape[0]
    first = mt_ref.shape[0] - peers * BR
    per = 256 // BR

    def remote(k, carry):
        rows = pl.ds(pl.multiple_of(first + k * 256, 256), 256)
        piece = jnp.dot(mt_ref[rows, :], grads, preferred_element_type=F32).astype(BF)
        out_ref[pl.ds(k * per, per), 0:BR, :] = piece.reshape(per, BR, width)
        return carry

    lax.fori_loop(0, peers // per, remote, 0)
    for d in range(peers):
        write_chunk(out_ref, (d,), BR, keep_ref[d].astype(F32) + got_ref[d].astype(F32))


def split(wide):
    top = wide.astype(BF)
    rest = (wide - top.astype(F32)).astype(BF)
    return jnp.concatenate([top, rest], axis=1)


def write_chunk(ref, at, first, total):
    ref[at + (slice(first, first + 16), slice(None))] = total[0:16].astype(BF)
    wide = split(total[16:24, 0:128] + total[16:24, 128:256])
    ref[at + (slice(first + 16, first + 24), slice(None))] = wide


def sum_body(first, in_ref, out_ref):
    total = in_ref[0, first : first + CHUNK, :].astype(F32)
    for s in range(1, in_ref.shape[0]):
        total += in_ref[s, first : first + CHUNK, :].astype(F32)
    for d in range(out_ref.shape[0]):
        write_chunk(out_ref, (d,), 0, total)


def gather_body(req_ref, local_ref, back_ref, out_ref):
    out_ref[...] = local_ref[...]

    def one(p, carry):
        out_ref[req_ref[p]] += back_ref[p, 0:BR, :].astype(F32)
        return carry

    lax.fori_loop(0, back_ref.shape[0], one, 0)


def finish_body(meta_ref, acc_ref, mine_ref, other_ref, out_ref, w_ref):
    out_ref[...] = acc_ref[...]
    core = meta_ref[0]
    hubs = mine_ref.shape[0] // 2
    for h in range(hubs):
        block = meta_ref[1 + h]

        @pl.when(block >= 0)
        def _():
            for ref, part in ((mine_ref, core), (other_ref, 1 - core)):
                for j in range(2):
                    rows = pl.ds(pl.multiple_of(part * HALF + j * 16, 16), 16)
                    out_ref[block, rows, :] += ref[2 * h + j, 0:16, :].astype(F32)

    half = w_ref.shape[0] // 2
    for ref, part in ((mine_ref, core), (other_ref, 1 - core)):
        for d in range(ref.shape[0]):
            pair = ref[d, 16:24, :].astype(F32)
            rows = pl.ds(pl.multiple_of(part * half + (d // 2) * 8, 8), 8)
            w_ref[rows, (d % 2) * 128 : (d % 2) * 128 + 128] = pair[:, 0:128] + pair[:, 128:256]


def shards(features, weight, cotangent, edge_source, edge_mult, read_blocks, hub_blocks):
    per_dev, width = features.shape
    blocks_dev = per_dev // BR
    hubs = hub_blocks.shape[0]
    slots = edge_source.shape[1]
    n_blk, n_z = lax.axis_size("blk"), lax.axis_size("z")
    blk, z, core = lax.axis_index("blk"), lax.axis_index("z"), lax.axis_index("core")
    shape = jax.ShapeDtypeStruct
    exchange = functools.partial(lax.all_to_all, split_axis=0, concat_axis=0, tiled=True)
    swap = functools.partial(lax.ppermute, axis_name="core", perm=[(0, 1), (1, 0)])

    hub_device = hub_blocks // blocks_dev
    hub_local = hub_blocks % blocks_dev
    hub_blk = hub_device // (2 * n_z)
    hub_z = (hub_device // 2) % n_z
    hub_core = hub_device % 2
    device = (blk * n_z + z) * 2 + core

    own_blocks = features.reshape(blocks_dev, BR, width)
    wanted = read_blocks.reshape(-1)

    own_halves = own_blocks.reshape(blocks_dev, 2, HALF, width)
    kept = lax.dynamic_index_in_dim(own_halves, core, 1, keepdims=False)
    got = swap(lax.dynamic_index_in_dim(own_halves, 1 - core, 1, keepdims=False))
    where_half = (hub_core ^ core) * blocks_dev + hub_local
    offered, token = call(
        offer_body, [shape((n_blk, CHUNK, width), BF), shape((8, 128), F32)], [SMEM, SMEM, VMEM, VMEM]
    )(where_half, wanted, kept, got)
    pieces = exchange(offered, "blk")

    n_half = hubs * HALF
    hub_row = edge_source - per_dev
    part = ((hub_row // HALF) % 2) ^ core
    moved = per_dev + part * n_half + (hub_row // BR) * HALF + hub_row % HALF
    is_hub = (hub_row >= 0) & (hub_row < 2 * n_half)
    column = jnp.where(is_hub, moved, edge_source)
    groups = per_dev // GROUP
    table_rows = per_dev + 2 * n_half + n_blk * BR
    dense, dense_t, inv = call(
        build_body,
        [
            shape((groups, GROUP, table_rows), BF),
            shape((table_rows, per_dev), BF),
            shape((groups, GROUP, 128), F32),
        ],
        [VMEM, VMEM, VMEM],
        flops=10**10,
        traffic=8 << 20,
        limit=16,
    )(column.reshape(groups, 1, GROUP * slots), edge_mult.reshape(groups, 1, GROUP * slots), token)
    dense = dense.reshape(per_dev, table_rows)
    inv = inv.reshape(per_dev, 128)

    here = blk // 2
    to_z = call(spread_body, shape((n_z, 16, width), BF), [SMEM, VMEM, ANY])(
        lax.dynamic_slice_in_dim(hub_blk, here, 1), pieces, inv
    )
    along = exchange(to_z, "z")
    requested = pieces[:, 16, 0].astype(jnp.int32)
    served = call(serve_body, shape((n_blk, BR + 16, width), BF), [SMEM, SMEM, VMEM, VMEM])(
        requested, lax.dynamic_slice_in_dim(hub_z, here, 1), own_blocks, along
    )
    incoming = exchange(served, "blk")
    hub_other = swap(incoming[:, BR:, :].reshape(-1, width))

    acc = call(
        first_body, shape((per_dev, width), F32), [VMEM] * 3, flops=10**9, traffic=6 << 20, limit=20
    )(dense, features, incoming)
    core_id = core.astype(jnp.int32).reshape(1)
    output, scaled, keep, send = call(
        layer_body,
        [shape((per_dev, width), BF)] * 2 + [shape((n_blk, CHUNK, width), BF)] * 2,
        [SMEM] + [VMEM] * 7,
        scratch=[pltpu.VMEM((per_dev, width), BF)] * 2 + [pltpu.VMEM((width, width), F32)],
        flops=10**9,
        traffic=6 << 20,
        limit=20,
    )(core_id, acc, dense, dense_t, inv, hub_other, weight, cotangent)
    local_grad, grads = call(
        table_body,
        [shape((per_dev, width), F32), shape((n_blk, BR + CHUNK, width), BF)],
        [VMEM] * 4,
        flops=10**9,
        traffic=6 << 20,
        limit=20,
    )(dense_t, scaled, keep, swap(send))

    returned = exchange(grads, "blk")
    chunks = lambda n: shape((n, CHUNK, width), BF)
    by_z = exchange(call(functools.partial(sum_body, BR), chunks(n_z), [VMEM])(returned), "z")
    mine = exchange(call(functools.partial(sum_body, 0), chunks(n_blk), [VMEM])(by_z), "blk")
    other = swap(mine)

    so_far = call(gather_body, shape((blocks_dev, BR, width), F32), [SMEM, VMEM, VMEM], traffic=4 << 20)(
        requested, local_grad.reshape(blocks_dev, BR, width), returned
    )
    meta = jnp.concatenate([core_id, jnp.where(hub_device == device, hub_local, -1).astype(jnp.int32)])
    feature_grad, weight_grad = call(
        finish_body,
        [shape((blocks_dev, BR, width), F32), shape((width, width), F32)],
        [SMEM] + [VMEM] * 3,
    )(meta, so_far, mine, other)
    return output, feature_grad.reshape(per_dev, width), weight_grad


def solution(mesh):
    n_blk, n_rep = mesh.devices.shape
    fine = Mesh(mesh.devices.reshape(n_blk, n_rep // 2, 2), ("blk", "z", "core"))
    axes = ("blk", "z", "core")
    rows = P(axes, None)
    in_specs = (rows, P(), rows, rows, rows, P(axes, None, None), P())
    out_specs = (rows, rows, P())
    return jax.shard_map(shards, mesh=fine, in_specs=in_specs, out_specs=out_specs, check_vma=False)
```

time: 773 us -> 199 us (0.26)
  waiting for transfers between devices: 480 us -> 12 us
  other arithmetic: 55 us -> 1.6 us
  blocking collectives: 156 us -> 108 us
  local copies, waits for them, and re-layouts: 43.9 us -> 7.56 us
  starting transfers between devices: 14.8 us -> 44.4 us
  Pallas kernels: 0 us -> 23.3 us
  between operations: 14.3 us -> 0.9 us
    psum x1 -> x0, waiting for transfers between devices: 480 us -> none  [shards(): hub_total, weight_grad = lax.psum((hub_grad, local_wgrad), ('blk', 'rep'))]
    psum x1 -> x0, blocking collectives: 138 us -> none  [shards(): hub_rows = lax.psum(offered, ('blk', 'rep')).astype(jnp.bfloat16)]
    all_to_all x1 -> x4, blocking collectives: 18.9 us -> 108 us  [the longest x1 40.3 us: shards(): returned = exchange(grads, 'blk')]
    scatter-add x1 -> x0, other arithmetic: 46.6 us -> none  [shards(): jax.ops.segment_sum(terms.reshape(-1, width), edge_source.reshape(-1), nu...]
    gather x3 -> x0, local copies, waits for them, and re-layouts: 36.2 us -> none  [the longest x1 33.1 us: shards(): rows = table[edge_source]]
    ppermute x0 -> x4, starting transfers between devices: none -> 29 us  [the longest x1 12.4 us: shards(): swap(lax.dynamic_index_in_dim(own_halves, 1 - core, 1, keepdims=False))]
    pallas_call x0 -> x11, Pallas kernels: none -> 23.3 us  [the longest x1 9.74 us: shards(): call(build_body, [shape((groups, GROUP, table_rows), BF), shape((table_ro...]
    all_to_all x2, waiting for transfers between devices: 0.01 us -> 10 us  [the longest x1 8.86 us: shards(): along = exchange(to_z, 'z')]
  transfers between devices with their start and end apart: 3 -> 6, of which waited for: 1 -> 4; matrix products, arithmetic and copies ran while one was open for 1% -> 2% of each run, Pallas kernels for 0% -> 6%
where the time goes in v1:
time: 199 us; the launch traced here: 198 us
  blocking collectives  108 us (54%)
  starting transfers between devices  44.4 us (22%)
  Pallas kernels  23.3 us (12%)
  waiting for transfers between devices  12 us (6%)
  local copies, waits for them, and re-layouts  7.56 us (4%)
    all_to_all x1, blocking collectives, shards(): returned = exchange(grads, 'blk')  40.3 us
    all_to_all x1, blocking collectives, shards(): incoming = exchange(served, 'blk')  38.7 us
    all_to_all x1, blocking collectives, shards(): exchange(call(functools.partial(sum_body, 0), chunks(n_blk), [VMEM])(by_z...  15.7 us
    all_to_all x1, blocking collectives, shards(): exchange(call(functools.partial(sum_body, BR), chunks(n_z), [VMEM])(retur...  13.6 us
    ppermute x1, starting transfers between devices, shards(): swap(lax.dynamic_index_in_dim(own_halves, 1 - core, 1, keepdims=False))  12.4 us
    all_to_all x1, starting transfers between devices, shards(): along = exchange(to_z, 'z')  11.6 us
    pallas_call x1, Pallas kernels, shards(): call(build_body, [shape((groups, GROUP, table_rows), BF), shape((table_ro...  9.74 us
    all_to_all x1, waiting for transfers between devices, shards(): along = exchange(to_z, 'z')  8.86 us
  transfers between devices with their start and end apart: 6, of which 4 were waited for; matrix products, arithmetic and copies ran while one was open for 2% of the time, Pallas kernels for 6%

profile of v1, /device:TPU:1, one launch (start us, length us, event | category | flops | bytes accessed | tf_op | source)
XLA Modules:
  0.0 198.2 jit_solution(16719750691867981517)
XLA Ops:
  0.6 0.0 copy-start.8
  0.6 0.0 copy-start.7
  0.7 1.0 dynamic-slice_bitcast_fusion
  1.7 12.4 %collective-permute-start = (bf16[8,32,256]{2,1,0:T(8,128)(2,1)S(1)}, bf16[8,32,256]{2,1,0:T(8,128)(2,1)S(1)}, u32[]{:S(2)}, u32[]{:S(2)}) collective-permute-start(bf16[8,32,256]{2,1,0:T(8,128)(2,1)S(1)} %get-tuple-element.32), channel_id=1, source_target_pairs={{0,1},{1,0},{2,3},{3,2},{4,5},{5,4},{6,7},{7,6},{8,9},{9,8},{10,11... | collective-permute-start | bytes 393224 | tf_op jit(solution)/shard_map/ppermute | solution.py:251
  14.1 0.8 fusion.6
  14.9 0.1 copy.14
  15.1 0.2 reshape.49.idx_ref
  15.2 0.9 copy.15
  16.1 0.2 reshape.50.mult_ref
  16.3 0.0 copy-done.8
  16.3 0.6 dynamic_slice.16.which_ref
  16.9 0.0 collective-permute-done.got_ref
  16.9 1.4 shard_map.94
  18.3 3.9 %all-to-all-start = ((bf16[32,24,256]{2,1,0:T(8,128)(2,1)}), bf16[32,24,256]{2,1,0:T(8,128)(2,1)S(1)}, u32[]{:S(2)}, u32[]{:S(2)}) async-start(bf16[32,24,256]{2,1,0:T(8,128)(2,1)} %get-tuple-element.18), calls=%async_computation | async-start | bytes 786432 | tf_op jit(solution)/shard_map/all_to_all | solution.py:256
  22.2 0.0 copy-start.4
  22.2 9.7 %shard_map.95 = (bf16[32,16,3584]{2,1,0:T(8,128)(2,1)S(1)}, bf16[3584,512]{1,0:T(8,128)(2,1)S(1)}, f32[32,16,128]{2,1,0:T(8,128)S(1)}) custom-call(s32[32,1,256]{2,1,0:T(1,128)S(1)} %reshape.49.idx_ref, s32[32,1,256]{2,1,0:T(1,128)S(1)} %reshape.50.mult_ref, f32[8,128]{1,0:T(8,128)S(1)} %get-tuple-element.16._), custom_call_target="tpu_custom_call" | custom-call | flops 10000000000 | bytes 8388608 | tf_op jit(solution)/shard_map/pallas_call | solution.py:266
  31.9 0.0 copy-start
  32.0 1.8 copy-done
  33.7 1.8 copy-done.2
  35.6 1.1 all-to-all-done.source_ref
  36.7 1.3 shard_map.96
  38.0 11.6 %all-to-all-start.1 = ((bf16[12,16,256]{2,1,0:T(8,128)(2,1)}), bf16[12,16,256]{2,1,0:T(8,128)(2,1)S(1)}, u32[]{:S(2)}, u32[]{:S(2)}) async-start(bf16[12,16,256]{2,1,0:T(8,128)(2,1)} %shard_map.96), calls=%async_computation.1 | async-start | bytes 196608 | tf_op jit(solution)/shard_map/all_to_all | solution.py:285
  49.6 0.6 dynamic_slice.15.hub_ref
  50.2 0.7 fusion.14.which_ref.req_ref
  50.9 8.9 %all-to-all-done.1.pieces_ref = bf16[12,16,256]{2,1,0:T(8,128)(2,1)S(1)} async-done(((bf16[12,16,256]{2,1,0:T(8,128)(2,1)}), bf16[12,16,256]{2,1,0:T(8,128)(2,1)S(1)}, u32[]{:S(2)}, u32[]{:S(2)}) %all-to-all-start.1) | async-done | bytes 98336 | tf_op jit(solution)/shard_map/all_to_all | solution.py:285
  59.7 1.4 shard_map.97
  61.2 38.7 %all_to_all.30.in_ref = bf16[32,80,256]{2,1,0:T(8,128)(2,1)S(1)} all-to-all(bf16[32,80,256]{2,1,0:T(8,128)(2,1)S(1)} %shard_map.97), channel_id=1, replica_groups=mesh['blk'=32,'z'=12,'core'=2] {'blk'}, dimensions={0} | all-to-all | bytes 2621440 | tf_op jit(solution)/shard_map/all_to_all | solution.py:290
  99.9 7.4 %collective-permute-start.1 = (bf16[512,256]{1,0:T(8,128)(2,1)S(1)}, bf16[512,256]{1,0:T(8,128)(2,1)S(1)}, u32[]{:S(2)}, u32[]{:S(2)}) collective-permute-start(bf16[512,256]{1,0:T(8,128)(2,1)S(1)} %bitcast.25), channel_id=1, source_target_pairs={{0,1},{1,0},{2,3},{3,2},{4,5},{5,4},{6,7},{7,6},{8,9},{9,8},{10,11... | collective-permute-start | bytes 786440 | tf_op jit(solution)/shard_map/ppermute | solution.py:291
  107.4 0.0 copy-start.5
  107.4 0.0 copy-start.6
  107.4 1.6 shard_map.98.acc_ref
  109.0 0.0 collective-permute-done.1.hub_ref
  109.0 0.3 copy-done.1
  109.4 0.0 copy-done.5
  109.4 0.0 copy-done.6
  109.4 3.0 %shard_map.99 = (bf16[512,256]{1,0:T(8,128)(2,1)}, bf16[512,256]{1,0:T(8,128)(2,1)S(1)}, bf16[32,24,256]{2,1,0:T(8,128)(2,1)S(1)}, bf16[32,24,256]{2,1,0:T(8,128)(2,1)S(1)}) custom-call(s32[1]{0:T(128)} %bitcast.core_ref, f32[512,256]{1,0:T(8,128)S(1)} %shard_map.98.acc_ref, bf16[512,3584]{1,0:T(8,128)(2,1)S(1)} %bitcast.18, ...), custom_call_target="tpu_custom_call" | custom-call | flops 1000000000 | bytes 6291456 | tf_op jit(solution)/shard_map/pallas_call | solution.py:297
  112.5 1.9 collective-permute-start.2
  114.4 1.7 collective-permute-done.2.got_ref
  116.1 2.2 %shard_map.100 = (f32[512,256]{1,0:T(8,128)S(1)}, bf16[32,88,256]{2,1,0:T(8,128)(2,1)S(1)}) custom-call(bf16[3584,512]{1,0:T(8,128)(2,1)S(1)} %copy-done.1, bf16[512,256]{1,0:T(8,128)(2,1)S(1)} %get-tuple-element.22.gs_ref, bf16[32,24,256]{2,1,0:T(8,128)(2,1)S(1)} %get-tuple-element.23.keep_ref, bf16[32,24,256]{2,1,0:T(8,128)(2,1)S(1)} %collective-permute-done.2.got_ref), custom_call_target="tpu_custom_call" | custom-call | flops 1000000000 | bytes 6291456 | tf_op jit(solution)/shard_map/pallas_call | solution.py:306
  118.3 40.3 %all_to_all.31.back_ref.in_ref = bf16[32,88,256]{2,1,0:T(8,128)(2,1)S(1)} all-to-all(bf16[32,88,256]{2,1,0:T(8,128)(2,1)S(1)} %get-tuple-element.26), channel_id=1, replica_groups=mesh['blk'=32,'z'=12,'core'=2] {'blk'}, dimensions={0} | all-to-all | bytes 2883584 | tf_op jit(solution)/shard_map/all_to_all | solution.py:315
  158.6 0.1 shard_map.102
  158.7 13.6 %all_to_all.32.in_ref = bf16[12,24,256]{2,1,0:T(8,128)(2,1)S(1)} all-to-all(bf16[12,24,256]{2,1,0:T(8,128)(2,1)S(1)} %shard_map.102), channel_id=1, replica_groups=mesh['blk'=32,'z'=12,'core'=2] {'z'}, dimensions={0} | all-to-all | bytes 294912 | tf_op jit(solution)/shard_map/all_to_all | solution.py:317
  172.4 15.7 %all_to_all.33.mine_ref = bf16[32,24,256]{2,1,0:T(8,128)(2,1)S(1)} all-to-all(bf16[32,24,256]{2,1,0:T(8,128)(2,1)S(1)} %shard_map.103), channel_id=1, replica_groups=mesh['blk'=32,'z'=12,'core'=2] {'blk'}, dimensions={0} | all-to-all | bytes 786432 | tf_op jit(solution)/shard_map/all_to_all | solution.py:318
  188.1 7.2 %collective-permute-start.3 = (bf16[32,24,256]{2,1,0:T(8,128)(2,1)S(1)}, bf16[32,24,256]{2,1,0:T(8,128)(2,1)S(1)}, u32[]{:S(2)}, u32[]{:S(2)}) collective-permute-start(bf16[32,24,256]{2,1,0:T(8,128)(2,1)S(1)} %all_to_all.33.mine_ref), channel_id=1, source_target_pairs={{0,1},{1,0},{2,3},{3,2},{4,5},{5,4},{6,7},{7,6},{8,9},{9,8},{10,11... | collective-permute-start | bytes 1179656 | tf_op jit(solution)/shard_map/ppermute | solution.py:319
  195.3 0.1 pad_add_fusion.meta_ref
  195.4 0.9 shard_map.101.acc_ref
  196.3 0.3 collective-permute-done.3.other_ref
  196.6 1.6 shard_map.104
  (10 shorter events, 0.1 us)
Async XLA Ops:
  0.6 15.7 %copy-start.8 = (s32[16]{0:T(128)S(1)}, s32[16]{0:T(128)}, u32[]{:S(2)}) copy-start(s32[16]{0:T(128)} %param.13) | copy-start | bytes 196
  0.6 16.3 %copy-start.7 = (s32[1,32,1]{1,2,0:T(1,128)S(1)}, s32[1,32,1]{1,2,0:T(1,128)}, u32[]{:S(2)}) copy-start(s32[1,32,1]{1,2,0:T(1,128)} %param.12) | copy-start | bytes 388
  1.7 15.3 %collective-permute-start = (bf16[8,32,256]{2,1,0:T(8,128)(2,1)S(1)}, bf16[8,32,256]{2,1,0:T(8,128)(2,1)S(1)}, u32[]{:S(2)}, u32[]{:S(2)}) collective-permute-start(bf16[8,32,256]{2,1,0:T(8,128)(2,1)S(1)} %get-tuple-element.32), channel_id=1, source_target_pairs={{0,1},{1,0},{2,3},{3,2},{4,5},{5,4},{6,7},{7,6},{8,9},{9,8},{10,11... | collective-permute-start | bytes 393224 | tf_op jit(solution)/shard_map/ppermute | solution.py:251
  18.3 18.4 %all-to-all-start = ((bf16[32,24,256]{2,1,0:T(8,128)(2,1)}), bf16[32,24,256]{2,1,0:T(8,128)(2,1)S(1)}, u32[]{:S(2)}, u32[]{:S(2)}) async-start(bf16[32,24,256]{2,1,0:T(8,128)(2,1)} %get-tuple-element.18), calls=%async_computation | async-start | bytes 786432 | tf_op jit(solution)/shard_map/all_to_all | solution.py:256
  22.2 37.5 %copy-start.4 = (bf16[512,256]{1,0:T(8,128)(2,1)S(1)}, bf16[512,256]{1,0:T(8,128)(2,1)}, u32[]{:S(2)}) copy-start(bf16[512,256]{1,0:T(8,128)(2,1)} %feat_ref.1) | copy-start | bytes 786436
  31.9 1.8 copy-start
  33.7 1.8 copy-start.2
  38.0 21.7 %all-to-all-start.1 = ((bf16[12,16,256]{2,1,0:T(8,128)(2,1)}), bf16[12,16,256]{2,1,0:T(8,128)(2,1)S(1)}, u32[]{:S(2)}, u32[]{:S(2)}) async-start(bf16[12,16,256]{2,1,0:T(8,128)(2,1)} %shard_map.96), calls=%async_computation.1 | async-start | bytes 196608 | tf_op jit(solution)/shard_map/all_to_all | solution.py:285
  59.7 47.6 %copy-start.3 = (bf16[32,16,3584]{2,1,0:T(8,128)(2,1)S(1)}, bf16[32,16,3584]{2,1,0:T(8,128)(2,1)}, u32[]{:S(2)}) copy-start(bf16[32,16,3584]{2,1,0:T(8,128)(2,1)} %copy-done.2) | copy-start | bytes 11010052
  99.9 9.1 %collective-permute-start.1 = (bf16[512,256]{1,0:T(8,128)(2,1)S(1)}, bf16[512,256]{1,0:T(8,128)(2,1)S(1)}, u32[]{:S(2)}, u32[]{:S(2)}) collective-permute-start(bf16[512,256]{1,0:T(8,128)(2,1)S(1)} %bitcast.25), channel_id=1, source_target_pairs={{0,1},{1,0},{2,3},{3,2},{4,5},{5,4},{6,7},{7,6},{8,9},{9,8},{10,11... | collective-permute-start | bytes 786440 | tf_op jit(solution)/shard_map/ppermute | solution.py:291
  107.3 2.0 %copy-start.1 = (bf16[3584,512]{1,0:T(8,128)(2,1)S(1)}, bf16[3584,512]{1,0:T(8,128)(2,1)}, u32[]{:S(2)}) copy-start(bf16[3584,512]{1,0:T(8,128)(2,1)} %copy-done) | copy-start | bytes 11010052
  107.4 2.0 %copy-start.5 = (bf16[512,256]{1,0:T(8,128)(2,1)S(1)}, bf16[512,256]{1,0:T(8,128)(2,1)}, u32[]{:S(2)}) copy-start(bf16[512,256]{1,0:T(8,128)(2,1)} %cot_ref.1) | copy-start | bytes 786436
  107.4 2.1 %copy-start.6 = (bf16[256,256]{1,0:T(8,128)(2,1)S(1)}, bf16[256,256]{1,0:T(8,128)(2,1)}, u32[]{:S(2)}) copy-start(bf16[256,256]{1,0:T(8,128)(2,1)} %weight_ref.1) | copy-start | bytes 393220
  112.5 3.6 %collective-permute-start.2 = (bf16[32,24,256]{2,1,0:T(8,128)(2,1)S(1)}, bf16[32,24,256]{2,1,0:T(8,128)(2,1)S(1)}, u32[]{:S(2)}, u32[]{:S(2)}) collective-permute-start(bf16[32,24,256]{2,1,0:T(8,128)(2,1)S(1)} %get-tuple-element.24), channel_id=1, source_target_pairs={{0,1},{1,0},{2,3},{3,2},{4,5},{5,4},{6,7},{7,6},{8,9},{9,8},{10,11... | collective-permute-start | bytes 1179656 | tf_op jit(solution)/shard_map/ppermute | solution.py:313
  188.1 8.5 %collective-permute-start.3 = (bf16[32,24,256]{2,1,0:T(8,128)(2,1)S(1)}, bf16[32,24,256]{2,1,0:T(8,128)(2,1)S(1)}, u32[]{:S(2)}, u32[]{:S(2)}) collective-permute-start(bf16[32,24,256]{2,1,0:T(8,128)(2,1)S(1)} %all_to_all.33.mine_ref), channel_id=1, source_target_pairs={{0,1},{1,0},{2,3},{3,2},{4,5},{5,4},{6,7},{7,6},{8,9},{9,8},{10,11... | collective-permute-start | bytes 1179656 | tf_op jit(solution)/shard_map/ppermute | solution.py:319

commit v2 on v1

v2 whole, which is shorter than its diff:
```python
import functools

import jax
import jax.numpy as jnp
from jax import lax
from jax.experimental import pallas as pl
from jax.experimental.pallas import tpu as pltpu
from jax.sharding import Mesh, PartitionSpec as P

BR = 64
PER_DEV = 512
HALF = BR // 2
GROUP = 16
CHUNK = 24
BF = jnp.bfloat16
F32 = jnp.float32
NT = (((1,), (1,)), ((), ()))
TN = (((0,), (0,)), ((), ()))
VMEM = pl.BlockSpec(memory_space=pltpu.VMEM)
SMEM = pl.BlockSpec(memory_space=pltpu.SMEM)
ANY = pl.BlockSpec(memory_space=pl.ANY)


def call(body, out, in_specs, scratch=(), flops=0, traffic=1 << 20, limit=8, outs=None):
    several = isinstance(out, (list, tuple))
    out_specs = outs or ([VMEM] * len(out) if several else VMEM)
    return pl.pallas_call(
        body,
        out_shape=out,
        in_specs=in_specs,
        out_specs=out_specs,
        scratch_shapes=list(scratch),
        compiler_params=pltpu.CompilerParams(vmem_limit_bytes=limit << 20),
        cost_estimate=pl.CostEstimate(flops=flops, bytes_accessed=traffic, transcendentals=0),
    )


def build_body(core_ref, idx_ref, mult_ref, main_ref, hub_ref, inv_ref, main_s, sems):
    groups, _, lanes = idx_ref.shape
    hub_cols = hub_ref.shape[2] // 128
    cols = main_ref.shape[2] // 128 + hub_cols
    first = PER_DEV // 128
    n_half = hub_cols * 64
    core = core_ref[0]
    own = (lax.broadcasted_iota(jnp.int32, (GROUP, lanes), 1) // 16) == lax.broadcasted_iota(
        jnp.int32, (GROUP, lanes), 0
    )
    low = lax.broadcasted_iota(jnp.int32, (128, lanes), 0)

    def group(g, carry):
        idx = idx_ref[g]
        row = idx - PER_DEV
        moved = PER_DEV + (((row >> 5) & 1) ^ core) * n_half + (row >> 6) * HALF + (row & (HALF - 1))
        idx = jnp.where((row >= 0) & (row < 2 * n_half), moved, idx)
        high = idx >> 7
        onehot = jnp.where(low == (idx & 127), 1.0, 0.0).astype(BF)
        mult = jnp.where(own, mult_ref[g].astype(F32), 0.0)
        inv_ref[g] = jnp.broadcast_to(1.0 / jnp.sum(mult, axis=1, keepdims=True), (GROUP, 128))
        left = jnp.concatenate([jnp.where(high == k, mult, 0.0).astype(BF) for k in range(cols)], axis=0)
        dense = lax.dot_general(left, onehot, NT, preferred_element_type=F32).astype(BF)
        for k in range(cols):
            tile = dense[k * GROUP : (k + 1) * GROUP]
            if first <= k < first + hub_cols:
                hub_ref[g, :, (k - first) * 128 : (k - first + 1) * 128] = tile
            else:
                at = k if k < first else k - hub_cols
                main_s[g, :, at * 128 : (at + 1) * 128] = tile
        return carry

    parts = sems.shape[0]
    per = groups // parts
    copies = []
    for q in range(parts):
        lax.fori_loop(q * per, (q + 1) * per, group, 0, unroll=4)
        rows = pl.ds(q * per, per)
        copies.append(pltpu.make_async_copy(main_s.at[rows], main_ref.at[rows], sems.at[q]))
        copies[-1].start()
    for copy in copies:
        copy.wait()


def offer_body(which_ref, wanted_ref, kept_ref, got_ref, out_ref):
    rows = kept_ref.shape[0]
    for h in range(out_ref.shape[0] // 2):
        at = which_ref[h]
        inner = jnp.where(at < rows, at, at - rows)
        block = jnp.where(at < rows, kept_ref[inner], got_ref[inner])
        for j in range(2):
            p = 2 * h + j
            out_ref[p, 0:16, :] = block[j * 16 : j * 16 + 16]
            out_ref[p, 16:24, :] = jnp.full((8, out_ref.shape[2]), wanted_ref[p].astype(F32), F32).astype(BF)


def pick_body(which_ref, here_ref, hub_blk_ref, blocks_ref, pieces_ref, _, out_ref, piece_ref):
    piece_ref[...] = pieces_ref[hub_blk_ref[here_ref[0]], 0:16, :]
    for i in range(out_ref.shape[0]):
        out_ref[i] = blocks_ref[which_ref[i]]


def spread_body(here_ref, hub_z_ref, source_ref, _, out_ref):
    chosen = source_ref[hub_z_ref[here_ref[0]]]
    for i in range(out_ref.shape[0]):
        out_ref[i] = chosen


def first_body(m_ref, feat_ref, in_ref, _, acc_ref):
    step = 128
    per_dev = feat_ref.shape[0]
    first = m_ref.shape[1] - in_ref.shape[0]

    def rows_of(i, carry):
        rows = pl.ds(pl.multiple_of(i * step, step), step)
        total = jnp.dot(m_ref[rows, 0:per_dev], feat_ref[...], preferred_element_type=F32)
        total += jnp.dot(m_ref[rows, first:], in_ref[...], preferred_element_type=F32)
        acc_ref[rows, :] = total
        return carry

    lax.fori_loop(0, per_dev // step, rows_of, 0)


def layer_body(core_ref, acc_ref, m_ref, inv_ref, mine_ref, other_ref, weight_ref, cot_ref,
               out_ref, gs_ref, keep_ref, send_ref, agg_s, pg_s, w_s):
    step = 128
    per_dev, width = acc_ref.shape
    n_half = mine_ref.shape[0]

    def rows_of(i, carry):
        rows = pl.ds(pl.multiple_of(i * step, step), step)
        total = acc_ref[rows, :]
        for base, ref in ((0, mine_ref), (n_half, other_ref)):
            total += jnp.dot(m_ref[rows, base : base + n_half], ref[...], preferred_element_type=F32)
        inv = inv_ref[rows, :]
        inv = jnp.concatenate([inv] * (width // 128), axis=1)
        agg = (total * inv).astype(BF)
        agg_s[rows, :] = agg
        pre = jnp.dot(agg, weight_ref[...], preferred_element_type=F32)
        sig = jax.nn.sigmoid(pre)
        out_ref[rows, :] = (pre * sig).astype(BF)
        slope = sig * (1.0 + pre * (1.0 - sig))
        pg = (cot_ref[rows, :].astype(F32) * slope).astype(BF)
        pg_s[rows, :] = pg
        ag = lax.dot_general(pg, weight_ref[...], NT, preferred_element_type=F32).astype(BF)
        gs_ref[rows, :] = (ag.astype(F32) * inv).astype(BF)
        return carry

    lax.fori_loop(0, per_dev // step, rows_of, 0)
    grads = gs_ref[...]
    w_s[...] = lax.dot_general(agg_s[...], pg_s[...], TN, preferred_element_type=F32)
    half = width // 2
    core = core_ref[0]
    for ref, base, part in ((send_ref, n_half, 1 - core), (keep_ref, 0, core)):
        for k in range(n_half // 256):
            cols = m_ref[:, base + k * 256 : base + (k + 1) * 256]
            piece = lax.dot_general(cols, grads, TN, preferred_element_type=F32).astype(BF)
            ref[k * 16 : (k + 1) * 16, 0:16, :] = piece.reshape(16, 16, width)
        wide = w_s[pl.ds(pl.multiple_of(part * half, half), half), :]
        for d in range(ref.shape[0]):
            tile = wide[(d // 2) * 8 : (d // 2) * 8 + 8, (d % 2) * 128 : (d % 2) * 128 + 128]
            ref[d, 16:24, :] = split(tile)


def table_body(m_ref, gs_ref, local_ref, remote_ref):
    grads = gs_ref[...]
    per_dev = local_ref.shape[0]
    for k in range(m_ref.shape[1] // 256):
        rows = slice(k * 256, (k + 1) * 256)
        piece = lax.dot_general(m_ref[:, rows], grads, TN, preferred_element_type=F32)
        if k < per_dev // 256:
            local_ref[rows, :] = piece
        else:
            remote_ref[k * 256 - per_dev : (k + 1) * 256 - per_dev, :] = piece.astype(BF)


def split(wide):
    top = wide.astype(BF)
    rest = (wide - top.astype(F32)).astype(BF)
    return jnp.concatenate([top, rest], axis=1)


def write_chunk(ref, at, total):
    ref[at + (slice(0, 16), slice(None))] = total[0:16].astype(BF)
    ref[at + (slice(16, 24), slice(None))] = split(total[16:24, 0:128] + total[16:24, 128:256])


def pair_body(keep_ref, got_ref, out_ref):
    for d in range(out_ref.shape[0]):
        write_chunk(out_ref, (d,), keep_ref[d].astype(F32) + got_ref[d].astype(F32))


def sum_body(in_ref, *refs):
    out_ref = refs[-1]
    total = in_ref[0].astype(F32)
    for s in range(1, in_ref.shape[0]):
        total += in_ref[s].astype(F32)
    if len(out_ref.shape) == 2:
        write_chunk(out_ref, (), total)
    else:
        for d in range(out_ref.shape[0]):
            write_chunk(out_ref, (d,), total)


def alias_body(*refs):
    pass


def copy_body(value_ref, _, out_ref):
    out_ref[...] = value_ref[...]


def gather_body(req_ref, local_ref, back_ref, out_ref):
    out_ref[...] = local_ref[...]

    def one(p, carry):
        out_ref[req_ref[p]] += back_ref[p].astype(F32)
        return carry

    lax.fori_loop(0, back_ref.shape[0], one, 0)


def finish_body(meta_ref, acc_ref, mine_ref, other_ref, out_ref, w_ref):
    out_ref[...] = acc_ref[...]
    core = meta_ref[0]
    hubs = mine_ref.shape[0] // 2
    for h in range(hubs):
        block = meta_ref[1 + h]

        @pl.when(block >= 0)
        def _():
            for ref, part in ((mine_ref, core), (other_ref, 1 - core)):
                for j in range(2):
                    rows = pl.ds(pl.multiple_of(part * HALF + j * 16, 16), 16)
                    out_ref[block, rows, :] += ref[2 * h + j, 0:16, :].astype(F32)

    half = w_ref.shape[0] // 2
    for ref, part in ((mine_ref, core), (other_ref, 1 - core)):
        for d in range(ref.shape[0]):
            pair = ref[d, 16:24, :].astype(F32)
            rows = pl.ds(pl.multiple_of(part * half + (d // 2) * 8, 8), 8)
            w_ref[rows, (d % 2) * 128 : (d % 2) * 128 + 128] = pair[:, 0:128] + pair[:, 128:256]


def shards(features, weight, cotangent, edge_source, edge_mult, read_blocks, hub_blocks):
    per_dev, width = features.shape
    blocks_dev = per_dev // BR
    hubs = hub_blocks.shape[0]
    slots = edge_source.shape[1]
    n_blk, n_z = lax.axis_size("blk"), lax.axis_size("z")
    blk, z, core = lax.axis_index("blk"), lax.axis_index("z"), lax.axis_index("core")
    shape = jax.ShapeDtypeStruct
    exchange = functools.partial(lax.all_to_all, split_axis=0, concat_axis=0, tiled=True)
    swap = functools.partial(lax.ppermute, axis_name="core", perm=[(0, 1), (1, 0)])

    hub_device = hub_blocks // blocks_dev
    hub_local = hub_blocks % blocks_dev
    hub_blk = hub_device // (2 * n_z)
    hub_z = (hub_device // 2) % n_z
    hub_core = hub_device % 2
    device = (blk * n_z + z) * 2 + core

    own_blocks = features.reshape(blocks_dev, BR, width)
    wanted = read_blocks.reshape(-1)

    own_halves = own_blocks.reshape(blocks_dev, 2, HALF, width)
    kept = lax.dynamic_index_in_dim(own_halves, core, 1, keepdims=False)
    got = swap(lax.dynamic_index_in_dim(own_halves, 1 - core, 1, keepdims=False))
    where_half = (hub_core ^ core) * blocks_dev + hub_local
    offered = call(
        offer_body, shape((n_blk, CHUNK, width), BF), [SMEM, SMEM, VMEM, VMEM]
    )(where_half, wanted, kept, got)
    pieces = exchange(offered, "blk")

    n_half = hubs * HALF
    core_id = core.astype(jnp.int32).reshape(1)
    groups = per_dev // GROUP
    main_rows = per_dev + n_blk * BR
    main, dense_hub, inv = call(
        build_body,
        [
            shape((groups, GROUP, main_rows), BF),
            shape((groups, GROUP, 2 * n_half), BF),
            shape((groups, GROUP, 128), F32),
        ],
        [SMEM, VMEM, VMEM],
        scratch=[pltpu.VMEM((groups, GROUP, main_rows), BF), pltpu.SemaphoreType.DMA((4,))],
        flops=8 * 10**9,
        traffic=8 << 20,
        limit=16,
        outs=[pl.BlockSpec(memory_space=pltpu.HBM), VMEM, VMEM],
    )(core_id, edge_source.reshape(groups, 1, GROUP * slots), edge_mult.reshape(groups, 1, GROUP * slots))
    main = main.reshape(per_dev, main_rows)
    dense_hub = dense_hub.reshape(per_dev, 2 * n_half)
    inv = inv.reshape(per_dev, 128)

    here = (blk // 2).astype(jnp.int32).reshape(1)
    requested = pieces[:, 16, 0].astype(jnp.int32)
    outgoing, piece = call(
        pick_body,
        [shape((n_blk, BR, width), BF), shape((16, width), BF)],
        [SMEM] * 3 + [VMEM] * 2 + [ANY],
    )(requested, here, hub_blk, own_blocks, pieces, inv)
    incoming = exchange(outgoing, "blk").reshape(-1, width)
    along = lax.all_gather(piece, "z")
    to_blk = call(spread_body, shape((n_blk, 16, width), BF), [SMEM, SMEM, VMEM, ANY])(
        here, hub_z, along, incoming
    )
    acc = call(
        first_body, shape((per_dev, width), F32), [VMEM] * 3 + [ANY], flops=10**9, traffic=6 << 20, limit=20
    )(main, features, incoming, to_blk)
    hub_mine = call(copy_body, shape((hubs * HALF, width), BF), [VMEM, VMEM])(
        exchange(to_blk, "blk").reshape(-1, width), acc
    )
    hub_other = swap(hub_mine)

    output, scaled, keep, send = call(
        layer_body,
        [shape((per_dev, width), BF)] * 2 + [shape((n_blk, CHUNK, width), BF)] * 2,
        [SMEM] + [VMEM] * 7,
        scratch=[pltpu.VMEM((per_dev, width), BF)] * 2 + [pltpu.VMEM((width, width), F32)],
        flops=10**9,
        traffic=6 << 20,
        limit=20,
    )(core_id, acc, dense_hub, inv, hub_mine, hub_other, weight, cotangent)
    local_grad, remote_grad = call(
        table_body,
        [shape((per_dev, width), F32), shape((n_blk * BR, width), BF)],
        [VMEM, VMEM],
        flops=10**9,
        traffic=6 << 20,
        limit=20,
    )(main, scaled)

    chunk = shape((CHUNK, width), BF)
    chunks = shape((n_blk, CHUNK, width), BF)
    by_blk = exchange(call(pair_body, chunks, [VMEM, VMEM])(keep, swap(send)), "blk")
    part_sum = call(sum_body, chunk, [VMEM])(by_blk)
    remote_grad = pl.pallas_call(
        alias_body,
        out_shape=shape(remote_grad.shape, BF),
        in_specs=[ANY, VMEM],
        out_specs=ANY,
        input_output_aliases={0: 0},
    )(remote_grad, part_sum)
    returned = exchange(remote_grad.reshape(n_blk, BR, width), "blk")
    full_sum = call(sum_body, chunks, [VMEM, ANY])(lax.all_gather(part_sum, "z"), returned)
    mine = exchange(full_sum, "blk")
    other = swap(mine)

    so_far = call(gather_body, shape((blocks_dev, BR, width), F32), [SMEM, VMEM, VMEM], traffic=4 << 20)(
        requested, local_grad.reshape(blocks_dev, BR, width), returned
    )
    meta = jnp.concatenate([core_id, jnp.where(hub_device == device, hub_local, -1).astype(jnp.int32)])
    feature_grad, weight_grad = call(
        finish_body,
        [shape((blocks_dev, BR, width), F32), shape((width, width), F32)],
        [SMEM] + [VMEM] * 3,
    )(meta, so_far, mine, other)
    return output, feature_grad.reshape(per_dev, width), weight_grad


def solution(mesh):
    n_blk, n_rep = mesh.devices.shape
    fine = Mesh(mesh.devices.reshape(n_blk, n_rep // 2, 2), ("blk", "z", "core"))
    axes = ("blk", "z", "core")
    rows = P(axes, None)
    in_specs = (rows, P(), rows, rows, rows, P(axes, None, None), P())
    out_specs = (rows, rows, P())
    return jax.shard_map(shards, mesh=fine, in_specs=in_specs, out_specs=out_specs, check_vma=False)
```

time: 199 us -> 189 us (0.950)
  blocking collectives: 108 us -> 63.2 us
  waiting for transfers between devices: 12 us -> 34.2 us
  starting transfers between devices: 44.4 us -> 56.9 us
  local copies, waits for them, and re-layouts: 7.56 us -> 12.6 us
  Pallas kernels: 23.3 us -> 18.4 us
    all_to_all x4 -> x1, blocking collectives: 108 us -> 17.9 us  [shards(): mine = exchange(full_sum, 'blk')]
    all_gather x0 -> x2, blocking collectives: none -> 45.3 us  [the longest x1 25.6 us: shards(): along = lax.all_gather(piece, 'z')]
    all_to_all x1 -> x4, waiting for transfers between devices: 8.86 us -> 24.8 us  [the longest x1 11.6 us: shards(): exchange(call(pair_body, chunks, [VMEM, VMEM])(keep, swap(send)), 'blk')]
    all_to_all x1 -> x4, starting transfers between devices: 11.6 us -> 21.5 us  [the longest x1 8.92 us: shards(): exchange(to_blk, 'blk').reshape(-1, width)]
    unnamed x19 -> x32, local copies, waits for them, and re-layouts: 4.94 us -> 11.3 us
    pallas_call x8 -> x11, Pallas kernels: 17.8 us -> 12.5 us  [the longest x1 4.29 us: shards(): call(build_body, [shape((groups, GROUP, main_rows), BF), shape((groups, G...]
    all_to_all x1, waiting for transfers between devices: 1.14 us -> 6.27 us  [shards(): pieces = exchange(offered, 'blk')]
    ppermute x1, starting transfers between devices: 7.44 us -> 9.61 us  [shards(): hub_other = swap(hub_mine)]
  transfers between devices with their start and end apart: 6 -> 9, of which waited for: 4 -> 8; matrix products, arithmetic and copies ran while one was open for 2% -> 1% of each run, Pallas kernels for 6% -> 4%
where the time goes in v2:
time: 189 us; the launch traced here: 188 us
  blocking collectives  63.2 us (33%)
  starting transfers between devices  56.9 us (30%)
  waiting for transfers between devices  34.2 us (18%)
  Pallas kernels  18.4 us (10%)
  local copies, waits for them, and re-layouts  12.6 us (7%)
    all_gather x1, blocking collectives, shards(): along = lax.all_gather(piece, 'z')  25.6 us
    all_gather x1, blocking collectives, shards(): lax.all_gather(part_sum, 'z')  19.7 us
    all_to_all x1, blocking collectives, shards(): mine = exchange(full_sum, 'blk')  17.9 us
    ppermute x1, starting transfers between devices, shards(): swap(lax.dynamic_index_in_dim(own_halves, 1 - core, 1, keepdims=False))  12.4 us
    all_to_all x1, waiting for transfers between devices, shards(): exchange(call(pair_body, chunks, [VMEM, VMEM])(keep, swap(send)), 'blk')  11.6 us
    unnamed x32, local copies, waits for them, and re-layouts  11.3 us
    ppermute x1, starting transfers between devices, shards(): hub_other = swap(hub_mine)  9.61 us
    all_to_all x1, starting transfers between devices, shards(): exchange(to_blk, 'blk').reshape(-1, width)  8.92 us
  transfers between devices with their start and end apart: 9, of which 8 were waited for; matrix products, arithmetic and copies ran while one was open for 1% of the time, Pallas kernels for 4%

profile of v2, /device:TPU:1, one launch (start us, length us, event | category | flops | bytes accessed | tf_op | source)
XLA Modules:
  0.0 187.5 jit_solution(8232948093149964514)
XLA Ops:
  0.6 1.0 dynamic-slice_bitcast_fusion
  1.6 12.4 %collective-permute-start = (bf16[8,32,256]{2,1,0:T(8,128)(2,1)S(1)}, bf16[8,32,256]{2,1,0:T(8,128)(2,1)S(1)}, u32[]{:S(2)}, u32[]{:S(2)}) collective-permute-start(bf16[8,32,256]{2,1,0:T(8,128)(2,1)S(1)} %get-tuple-element.32), channel_id=1, source_target_pairs={{0,1},{1,0},{2,3},{3,2},{4,5},{5,4},{6,7},{7,6},{8,9},{9,8},{10,11... | collective-permute-start | bytes 393224 | tf_op jit(solution)/shard_map/ppermute | solution.py:265
  14.1 0.7 compare_select_fusion
  14.8 0.3 collective-permute-done.got_ref
  15.0 0.7 copy-done.7
  15.7 1.3 shard_map.95
  17.0 3.9 %all-to-all-start = ((bf16[32,24,256]{2,1,0:T(8,128)(2,1)}), bf16[32,24,256]{2,1,0:T(8,128)(2,1)S(1)}, u32[]{:S(2)}, u32[]{:S(2)}) async-start(bf16[32,24,256]{2,1,0:T(8,128)(2,1)} %shard_map.95), calls=%async_computation | async-start | bytes 786432 | tf_op jit(solution)/shard_map/all_to_all | solution.py:270
  20.9 0.9 copy.15
  21.8 0.2 reshape.67.idx_ref
  22.0 0.1 copy.16
  22.1 0.2 reshape.68.mult_ref
  22.3 4.3 %shard_map.94 = (bf16[32,16,2560]{2,1,0:T(8,128)(2,1)S(1)}, bf16[32,16,1024]{2,1,0:T(8,128)(2,1)S(1)}, f32[32,16,128]{2,1,0:T(8,128)S(1)}) custom-call(s32[1]{0:T(128)} %bitcast.core_ref, s32[32,1,256]{2,1,0:T(1,128)S(1)} %reshape.67.idx_ref, s32[32,1,256]{2,1,0:T(1,128)S(1)} %reshape.68.mult_ref), custom_call_target="tpu_custom_call" | custom-call | flops 8000000000 | bytes 8388608 | tf_op jit(solution)/shard_map/pallas_call | solution.py:276
  26.6 1.5 copy-done.1
  28.1 1.0 copy-done.10
  29.1 6.3 %all-to-all-done.pieces_ref = bf16[32,24,256]{2,1,0:T(8,128)(2,1)S(1)} async-done(((bf16[32,24,256]{2,1,0:T(8,128)(2,1)}), bf16[32,24,256]{2,1,0:T(8,128)(2,1)S(1)}, u32[]{:S(2)}, u32[]{:S(2)}) %all-to-all-start) | async-done | bytes 393248 | tf_op jit(solution)/shard_map/all_to_all | solution.py:270
  35.4 0.7 fusion.which_ref.req_ref
  36.0 1.6 shard_map.96
  37.6 4.4 %all-to-all-start.1 = ((bf16[32,64,256]{2,1,0:T(8,128)(2,1)}), bf16[32,64,256]{2,1,0:T(8,128)(2,1)S(1)}, u32[]{:S(2)}, u32[]{:S(2)}) async-start(bf16[32,64,256]{2,1,0:T(8,128)(2,1)} %get-tuple-element.18), calls=%async_computation.1 | async-start | bytes 2097152 | tf_op jit(solution)/shard_map/all_to_all | solution.py:301
  42.0 25.6 %all-gather = bf16[192,256]{1,0:T(8,128)(2,1)S(1)} all-gather(bf16[16,256]{1,0:T(8,128)(2,1)S(1)} %get-tuple-element.19), channel_id=2, replica_groups=mesh['blk'=32,'z'=12,'core'=2] {'z'}, dimensions={0}, use_global_device_ids=true | all-gather | bytes 106496 | tf_op jit(solution)/shard_map/all_gather | solution.py:302
  67.6 1.3 shard_map.97._
  68.9 8.9 %all-to-all-start.2 = ((bf16[32,16,256]{2,1,0:T(8,128)(2,1)}), bf16[32,16,256]{2,1,0:T(8,128)(2,1)S(1)}, u32[]{:S(2)}, u32[]{:S(2)}) async-start(bf16[32,16,256]{2,1,0:T(8,128)(2,1)} %shard_map.97._), calls=%async_computation.2 | async-start | bytes 524288 | tf_op jit(solution)/shard_map/all_to_all | solution.py:310
  77.8 1.7 copy-done.2
  79.6 1.4 shard_map.98._.acc_ref
  80.9 7.3 %all-to-all-done.2 = bf16[32,16,256]{2,1,0:T(8,128)(2,1)S(1)} async-done(((bf16[32,16,256]{2,1,0:T(8,128)(2,1)}), bf16[32,16,256]{2,1,0:T(8,128)(2,1)S(1)}, u32[]{:S(2)}, u32[]{:S(2)}) %all-to-all-start.2) | async-done | bytes 262176 | tf_op jit(solution)/shard_map/all_to_all | solution.py:310
  88.2 9.6 %collective-permute-start.1 = (bf16[512,256]{1,0:T(8,128)(2,1)S(1)}, bf16[512,256]{1,0:T(8,128)(2,1)S(1)}, u32[]{:S(2)}, u32[]{:S(2)}) collective-permute-start(bf16[512,256]{1,0:T(8,128)(2,1)S(1)} %shard_map.99.mine_ref), channel_id=1, source_target_pairs={{0,1},{1,0},{2,3},{3,2},{4,5},{5,4},{6,7},{7,6},{8,9},{9,8},{10,11... | collective-permute-start | bytes 786440 | tf_op jit(solution)/shard_map/ppermute | solution.py:312
  97.9 1.1 collective-permute-done.1.other_ref
  99.0 0.9 copy-done.8
  100.0 1.2 copy-done.11
  101.2 3.3 %shard_map.100 = (bf16[512,256]{1,0:T(8,128)(2,1)}, bf16[512,256]{1,0:T(8,128)(2,1)S(1)}, bf16[32,24,256]{2,1,0:T(8,128)(2,1)S(1)}, bf16[32,24,256]{2,1,0:T(8,128)(2,1)S(1)}) custom-call(s32[1]{0:T(128)} %bitcast.core_ref, f32[512,256]{1,0:T(8,128)S(1)} %shard_map.98._.acc_ref, bf16[512,1024]{1,0:T(8,128)(2,1)S(1)} %bitcast.37, f32[512,128]{1,0:T(8,128)S(1)} %bitcast.35, ...), custom_call_target="tpu_custom_call" | custom-call | flops 1000000000 | bytes 6291456 | tf_op jit(solution)/shard_map/pallas_call | solution.py:314
  104.5 0.7 copy-done.12
  105.2 2.3 %collective-permute-start.2 = (bf16[32,24,256]{2,1,0:T(8,128)(2,1)S(1)}, bf16[32,24,256]{2,1,0:T(8,128)(2,1)S(1)}, u32[]{:S(2)}, u32[]{:S(2)}) collective-permute-start(bf16[32,24,256]{2,1,0:T(8,128)(2,1)S(1)} %get-tuple-element.26), channel_id=1, source_target_pairs={{0,1},{1,0},{2,3},{3,2},{4,5},{5,4},{6,7},{7,6},{8,9},{9,8},{10,11... | collective-permute-start | bytes 1179656 | tf_op jit(solution)/shard_map/ppermute | solution.py:334
  107.5 1.3 collective-permute-done.2.got_ref
  108.8 0.9 shard_map.102
  109.7 3.9 %all-to-all-start.3 = ((bf16[32,24,256]{2,1,0:T(8,128)(2,1)}), bf16[32,24,256]{2,1,0:T(8,128)(2,1)S(1)}, u32[]{:S(2)}, u32[]{:S(2)}) async-start(bf16[32,24,256]{2,1,0:T(8,128)(2,1)} %shard_map.102), calls=%async_computation.3 | async-start | bytes 786432 | tf_op jit(solution)/shard_map/all_to_all | solution.py:334
  113.6 0.9 copy-done.13
  114.5 0.9 shard_map.101
  115.4 1.0 copy-done
  116.4 11.6 %all-to-all-done.3.in_ref = bf16[32,24,256]{2,1,0:T(8,128)(2,1)S(1)} async-done(((bf16[32,24,256]{2,1,0:T(8,128)(2,1)}), bf16[32,24,256]{2,1,0:T(8,128)(2,1)S(1)}, u32[]{:S(2)}, u32[]{:S(2)}) %all-to-all-start.3) | async-done | bytes 393248 | tf_op jit(solution)/shard_map/all_to_all | solution.py:334
  128.1 0.6 copy-done.5
  128.7 0.8 shard_map.104
  129.4 4.4 %all-to-all-start.4 = ((bf16[32,64,256]{2,1,0:T(8,128)(2,1)}), bf16[32,64,256]{2,1,0:T(8,128)(2,1)S(1)}, u32[]{:S(2)}, u32[]{:S(2)}) async-start(bf16[32,64,256]{2,1,0:T(8,128)(2,1)} %bitcast.25), calls=%async_computation.4 | async-start | bytes 2097152 | tf_op jit(solution)/shard_map/all_to_all | solution.py:343
  133.8 19.7 %all-gather.1 = bf16[288,256]{1,0:T(8,128)(2,1)S(1)} all-gather(bf16[24,256]{1,0:T(8,128)(2,1)S(1)} %copy-done.6), channel_id=3, replica_groups=mesh['blk'=32,'z'=12,'core'=2] {'z'}, dimensions={0}, use_global_device_ids=true | all-gather | bytes 159744 | tf_op jit(solution)/shard_map/all_gather | solution.py:344
  153.5 5.9 %all-to-all-done.4.back_ref.refs_0_ = bf16[32,64,256]{2,1,0:T(8,128)(2,1)S(1)} async-done(((bf16[32,64,256]{2,1,0:T(8,128)(2,1)}), bf16[32,64,256]{2,1,0:T(8,128)(2,1)S(1)}, u32[]{:S(2)}, u32[]{:S(2)}) %all-to-all-start.4) | async-done | bytes 1048608 | tf_op jit(solution)/shard_map/all_to_all | solution.py:343
  159.5 17.9 %all_to_all.30.mine_ref = bf16[32,24,256]{2,1,0:T(8,128)(2,1)S(1)} all-to-all(bf16[32,24,256]{2,1,0:T(8,128)(2,1)S(1)} %shard_map.106), channel_id=1, replica_groups=mesh['blk'=32,'z'=12,'core'=2] {'blk'}, dimensions={0} | all-to-all | bytes 786432 | tf_op jit(solution)/shard_map/all_to_all | solution.py:345
  177.4 7.2 %collective-permute-start.3 = (bf16[32,24,256]{2,1,0:T(8,128)(2,1)S(1)}, bf16[32,24,256]{2,1,0:T(8,128)(2,1)S(1)}, u32[]{:S(2)}, u32[]{:S(2)}) collective-permute-start(bf16[32,24,256]{2,1,0:T(8,128)(2,1)S(1)} %all_to_all.30.mine_ref), channel_id=1, source_target_pairs={{0,1},{1,0},{2,3},{3,2},{4,5},{5,4},{6,7},{7,6},{8,9},{9,8},{10,11... | collective-permute-start | bytes 1179656 | tf_op jit(solution)/shard_map/ppermute | solution.py:346
  184.7 0.9 shard_map.105.acc_ref
  185.6 0.3 collective-permute-done.3.other_ref
  185.9 1.6 shard_map.107
  (26 shorter events, 0.3 us)
Async XLA Ops:
  0.6 21.4 %copy-start.14 = (s32[512,16]{0,1:T(8,128)S(1)}, s32[512,16]{0,1:T(8,128)}, u32[]{:S(2)}) copy-start(s32[512,16]{0,1:T(8,128)} %param.11) | copy-start | bytes 98308
  1.6 13.4 %collective-permute-start = (bf16[8,32,256]{2,1,0:T(8,128)(2,1)S(1)}, bf16[8,32,256]{2,1,0:T(8,128)(2,1)S(1)}, u32[]{:S(2)}, u32[]{:S(2)}) collective-permute-start(bf16[8,32,256]{2,1,0:T(8,128)(2,1)S(1)} %get-tuple-element.32), channel_id=1, source_target_pairs={{0,1},{1,0},{2,3},{3,2},{4,5},{5,4},{6,7},{7,6},{8,9},{9,8},{10,11... | collective-permute-start | bytes 393224 | tf_op jit(solution)/shard_map/ppermute | solution.py:265
  15.0 0.7 copy-start.7
  17.0 18.3 %all-to-all-start = ((bf16[32,24,256]{2,1,0:T(8,128)(2,1)}), bf16[32,24,256]{2,1,0:T(8,128)(2,1)S(1)}, u32[]{:S(2)}, u32[]{:S(2)}) async-start(bf16[32,24,256]{2,1,0:T(8,128)(2,1)} %shard_map.95), calls=%async_computation | async-start | bytes 786432 | tf_op jit(solution)/shard_map/all_to_all | solution.py:270
  22.3 13.7 %copy-start.4 = (bf16[512,256]{1,0:T(8,128)(2,1)S(1)}, bf16[512,256]{1,0:T(8,128)(2,1)}, u32[]{:S(2)}) copy-start(bf16[512,256]{1,0:T(8,128)(2,1)} %feat_ref.1) | copy-start | bytes 786436
  26.6 1.5 copy-start.1
  28.1 1.0 copy-start.10
  37.6 30.0 %all-to-all-start.1 = ((bf16[32,64,256]{2,1,0:T(8,128)(2,1)}), bf16[32,64,256]{2,1,0:T(8,128)(2,1)S(1)}, u32[]{:S(2)}, u32[]{:S(2)}) async-start(bf16[32,64,256]{2,1,0:T(8,128)(2,1)} %get-tuple-element.18), calls=%async_computation.1 | async-start | bytes 2097152 | tf_op jit(solution)/shard_map/all_to_all | solution.py:301
  68.9 19.3 %all-to-all-start.2 = ((bf16[32,16,256]{2,1,0:T(8,128)(2,1)}), bf16[32,16,256]{2,1,0:T(8,128)(2,1)S(1)}, u32[]{:S(2)}, u32[]{:S(2)}) async-start(bf16[32,16,256]{2,1,0:T(8,128)(2,1)} %shard_map.97._), calls=%async_computation.2 | async-start | bytes 524288 | tf_op jit(solution)/shard_map/all_to_all | solution.py:310
  77.8 1.7 copy-start.2
  79.6 19.4 %copy-start.9 = (bf16[256,256]{1,0:T(8,128)(2,1)S(1)}, bf16[256,256]{1,0:T(8,128)(2,1)}, u32[]{:S(2)}) copy-start(bf16[256,256]{1,0:T(8,128)(2,1)} %weight_ref.1) | copy-start | bytes 393220
  88.2 10.8 %collective-permute-start.1 = (bf16[512,256]{1,0:T(8,128)(2,1)S(1)}, bf16[512,256]{1,0:T(8,128)(2,1)S(1)}, u32[]{:S(2)}, u32[]{:S(2)}) collective-permute-start(bf16[512,256]{1,0:T(8,128)(2,1)S(1)} %shard_map.99.mine_ref), channel_id=1, source_target_pairs={{0,1},{1,0},{2,3},{3,2},{4,5},{5,4},{6,7},{7,6},{8,9},{9,8},{10,11... | collective-permute-start | bytes 786440 | tf_op jit(solution)/shard_map/ppermute | solution.py:312
  99.0 1.0 copy-start.8
  100.0 1.2 copy-start.11
  101.2 12.4 %copy-start.3 = (bf16[32,16,2560]{2,1,0:T(8,128)(2,1)S(1)}, bf16[32,16,2560]{2,1,0:T(8,128)(2,1)}, u32[]{:S(2)}) copy-start(bf16[32,16,2560]{2,1,0:T(8,128)(2,1)} %copy-done.1) | copy-start | bytes 7864324
  104.5 0.7 copy-start.12
  105.2 3.6 %collective-permute-start.2 = (bf16[32,24,256]{2,1,0:T(8,128)(2,1)S(1)}, bf16[32,24,256]{2,1,0:T(8,128)(2,1)S(1)}, u32[]{:S(2)}, u32[]{:S(2)}) collective-permute-start(bf16[32,24,256]{2,1,0:T(8,128)(2,1)S(1)} %get-tuple-element.26), channel_id=1, source_target_pairs={{0,1},{1,0},{2,3},{3,2},{4,5},{5,4},{6,7},{7,6},{8,9},{9,8},{10,11... | collective-permute-start | bytes 1179656 | tf_op jit(solution)/shard_map/ppermute | solution.py:334
  109.7 18.3 %all-to-all-start.3 = ((bf16[32,24,256]{2,1,0:T(8,128)(2,1)}), bf16[32,24,256]{2,1,0:T(8,128)(2,1)S(1)}, u32[]{:S(2)}, u32[]{:S(2)}) async-start(bf16[32,24,256]{2,1,0:T(8,128)(2,1)} %shard_map.102), calls=%async_computation.3 | async-start | bytes 786432 | tf_op jit(solution)/shard_map/all_to_all | solution.py:334
  113.6 1.0 copy-start.13
  115.4 1.0 copy-start
  128.0 0.6 copy-start.5
  128.7 5.2 %copy-start.6 = (bf16[24,256]{1,0:T(8,128)(2,1)S(1)}, bf16[24,256]{1,0:T(8,128)(2,1)}, u32[]{:S(2)}) copy-start(bf16[24,256]{1,0:T(8,128)(2,1)} %copy-done.5) | copy-start | bytes 36868
  129.4 30.0 %all-to-all-start.4 = ((bf16[32,64,256]{2,1,0:T(8,128)(2,1)}), bf16[32,64,256]{2,1,0:T(8,128)(2,1)S(1)}, u32[]{:S(2)}, u32[]{:S(2)}) async-start(bf16[32,64,256]{2,1,0:T(8,128)(2,1)} %bitcast.25), calls=%async_computation.4 | async-start | bytes 2097152 | tf_op jit(solution)/shard_map/all_to_all | solution.py:343
  177.4 8.5 %collective-permute-start.3 = (bf16[32,24,256]{2,1,0:T(8,128)(2,1)S(1)}, bf16[32,24,256]{2,1,0:T(8,128)(2,1)S(1)}, u32[]{:S(2)}, u32[]{:S(2)}) collective-permute-start(bf16[32,24,256]{2,1,0:T(8,128)(2,1)S(1)} %all_to_all.30.mine_ref), channel_id=1, source_target_pairs={{0,1},{1,0},{2,3},{3,2},{4,5},{5,4},{6,7},{7,6},{8,9},{9,8},{10,11... | collective-permute-start | bytes 1179656 | tf_op jit(solution)/shard_map/ppermute | solution.py:346

commit v3 on v2

--- a/solution.py
+++ b/solution.py
@@ -11,7 +11,7 @@
 PER_DEV = 512
 HALF = BR // 2
 GROUP = 16
-CHUNK = 24
+CHUNK = 40
 BF = jnp.bfloat16
 F32 = jnp.float32
 NT = (((1,), (1,)), ((), ()))
@@ -79,6 +79,15 @@
         copy.wait()
 
 
+def put_rows(ref, at, rows):
+    ref[at, 0:16, :] = rows[:, 0:128]
+    ref[at, 16:32, :] = rows[:, 128:256]
+
+
+def get_rows(ref, at):
+    return jnp.concatenate([ref[at, 0:16, :], ref[at, 16:32, :]], axis=1)
+
+
 def offer_body(which_ref, wanted_ref, kept_ref, got_ref, out_ref):
     rows = kept_ref.shape[0]
     for h in range(out_ref.shape[0] // 2):
@@ -87,12 +96,12 @@
         block = jnp.where(at < rows, kept_ref[inner], got_ref[inner])
         for j in range(2):
             p = 2 * h + j
-            out_ref[p, 0:16, :] = block[j * 16 : j * 16 + 16]
-            out_ref[p, 16:24, :] = jnp.full((8, out_ref.shape[2]), wanted_ref[p].astype(F32), F32).astype(BF)
+            put_rows(out_ref, p, block[j * 16 : j * 16 + 16])
+            out_ref[p, 32:40, :] = jnp.full((8, 128), wanted_ref[p].astype(F32), F32).astype(BF)
 
 
 def pick_body(which_ref, here_ref, hub_blk_ref, blocks_ref, pieces_ref, _, out_ref, piece_ref):
-    piece_ref[...] = pieces_ref[hub_blk_ref[here_ref[0]], 0:16, :]
+    piece_ref[...] = get_rows(pieces_ref, hub_blk_ref[here_ref[0]])
     for i in range(out_ref.shape[0]):
         out_ref[i] = blocks_ref[which_ref[i]]
 
@@ -118,17 +127,31 @@
     lax.fori_loop(0, per_dev // step, rows_of, 0)
 
 
-def layer_body(core_ref, acc_ref, m_ref, inv_ref, mine_ref, other_ref, weight_ref, cot_ref,
-               out_ref, gs_ref, keep_ref, send_ref, agg_s, pg_s, w_s):
+def mid_body(m_ref, mine_ref, acc_ref, sum_ref, keep_ref):
+    step = 128
+    per_dev = acc_ref.shape[0]
+    n_half = mine_ref.shape[0]
+
+    def rows_of(i, carry):
+        rows = pl.ds(pl.multiple_of(i * step, step), step)
+        part = jnp.dot(m_ref[rows, 0:n_half], mine_ref[...], preferred_element_type=F32)
+        sum_ref[rows, :] = acc_ref[rows, :] + part
+        keep_ref[rows, :] = m_ref[rows, :]
+        return carry
+
+    lax.fori_loop(0, per_dev // step, rows_of, 0, unroll=2)
+
+
+def layer_body(core_ref, acc_ref, m_ref, inv_ref, other_ref, weight_ref, cot_ref,
+               out_ref, gs_out, keep_ref, send_ref, agg_s, pg_s, gs_ref, w_s, sem):
     step = 128
     per_dev, width = acc_ref.shape
-    n_half = mine_ref.shape[0]
+    n_half = other_ref.shape[0]
 
     def rows_of(i, carry):
         rows = pl.ds(pl.multiple_of(i * step, step), step)
         total = acc_ref[rows, :]
-        for base, ref in ((0, mine_ref), (n_half, other_ref)):
-            total += jnp.dot(m_ref[rows, base : base + n_half], ref[...], preferred_element_type=F32)
+        total += jnp.dot(m_ref[rows, n_half:], other_ref[...], preferred_element_type=F32)
         inv = inv_ref[rows, :]
         inv = jnp.concatenate([inv] * (width // 128), axis=1)
         agg = (total * inv).astype(BF)
@@ -143,7 +166,9 @@
         gs_ref[rows, :] = (ag.astype(F32) * inv).astype(BF)
         return carry
 
-    lax.fori_loop(0, per_dev // step, rows_of, 0)
+    lax.fori_loop(0, per_dev // step, rows_of, 0, unroll=2)
+    out_copy = pltpu.make_async_copy(gs_ref, gs_out, sem)
+    out_copy.start()
     grads = gs_ref[...]
     w_s[...] = lax.dot_general(agg_s[...], pg_s[...], TN, preferred_element_type=F32)
     half = width // 2
@@ -152,11 +177,14 @@
         for k in range(n_half // 256):
             cols = m_ref[:, base + k * 256 : base + (k + 1) * 256]
             piece = lax.dot_general(cols, grads, TN, preferred_element_type=F32).astype(BF)
-            ref[k * 16 : (k + 1) * 16, 0:16, :] = piece.reshape(16, 16, width)
+            piece = piece.reshape(16, 16, width)
+            ref[k * 16 : (k + 1) * 16, 0:16, :] = piece[:, :, 0:128]
+            ref[k * 16 : (k + 1) * 16, 16:32, :] = piece[:, :, 128:256]
         wide = w_s[pl.ds(pl.multiple_of(part * half, half), half), :]
         for d in range(ref.shape[0]):
             tile = wide[(d // 2) * 8 : (d // 2) * 8 + 8, (d % 2) * 128 : (d % 2) * 128 + 128]
-            ref[d, 16:24, :] = split(tile)
+            ref[d, 32:40, :] = tile.astype(BF)
+    out_copy.wait()
 
 
 def table_body(m_ref, gs_ref, local_ref, remote_ref):
@@ -171,20 +199,8 @@
             remote_ref[k * 256 - per_dev : (k + 1) * 256 - per_dev, :] = piece.astype(BF)
 
 
-def split(wide):
-    top = wide.astype(BF)
-    rest = (wide - top.astype(F32)).astype(BF)
-    return jnp.concatenate([top, rest], axis=1)
-
-
-def write_chunk(ref, at, total):
-    ref[at + (slice(0, 16), slice(None))] = total[0:16].astype(BF)
-    ref[at + (slice(16, 24), slice(None))] = split(total[16:24, 0:128] + total[16:24, 128:256])
-
-
 def pair_body(keep_ref, got_ref, out_ref):
-    for d in range(out_ref.shape[0]):
-        write_chunk(out_ref, (d,), keep_ref[d].astype(F32) + got_ref[d].astype(F32))
+    out_ref[...] = (keep_ref[...].astype(F32) + got_ref[...].astype(F32)).astype(BF)
 
 
 def sum_body(in_ref, *refs):
@@ -192,19 +208,7 @@
     total = in_ref[0].astype(F32)
     for s in range(1, in_ref.shape[0]):
         total += in_ref[s].astype(F32)
-    if len(out_ref.shape) == 2:
-        write_chunk(out_ref, (), total)
-    else:
-        for d in range(out_ref.shape[0]):
-            write_chunk(out_ref, (d,), total)
-
-
-def alias_body(*refs):
-    pass
-
-
-def copy_body(value_ref, _, out_ref):
-    out_ref[...] = value_ref[...]
+    out_ref[...] = jnp.broadcast_to(total.astype(BF), out_ref.shape)
 
 
 def gather_body(req_ref, local_ref, back_ref, out_ref):
@@ -229,14 +233,13 @@
             for ref, part in ((mine_ref, core), (other_ref, 1 - core)):
                 for j in range(2):
                     rows = pl.ds(pl.multiple_of(part * HALF + j * 16, 16), 16)
-                    out_ref[block, rows, :] += ref[2 * h + j, 0:16, :].astype(F32)
+                    out_ref[block, rows, :] += get_rows(ref, 2 * h + j).astype(F32)
 
     half = w_ref.shape[0] // 2
     for ref, part in ((mine_ref, core), (other_ref, 1 - core)):
         for d in range(ref.shape[0]):
-            pair = ref[d, 16:24, :].astype(F32)
             rows = pl.ds(pl.multiple_of(part * half + (d // 2) * 8, 8), 8)
-            w_ref[rows, (d % 2) * 128 : (d % 2) * 128 + 128] = pair[:, 0:128] + pair[:, 128:256]
+            w_ref[rows, (d % 2) * 128 : (d % 2) * 128 + 128] = ref[d, 32:40, :].astype(F32)
 
 
 def shards(features, weight, cotangent, edge_source, edge_mult, read_blocks, hub_blocks):
@@ -265,7 +268,7 @@
     got = swap(lax.dynamic_index_in_dim(own_halves, 1 - core, 1, keepdims=False))
     where_half = (hub_core ^ core) * blocks_dev + hub_local
     offered = call(
-        offer_body, shape((n_blk, CHUNK, width), BF), [SMEM, SMEM, VMEM, VMEM]
+        offer_body, shape((n_blk, CHUNK, 128), BF), [SMEM, SMEM, VMEM, VMEM]
     )(where_half, wanted, kept, got)
     pieces = exchange(offered, "blk")
 
@@ -282,8 +285,8 @@
         ],
         [SMEM, VMEM, VMEM],
         scratch=[pltpu.VMEM((groups, GROUP, main_rows), BF), pltpu.SemaphoreType.DMA((4,))],
-        flops=8 * 10**9,
-        traffic=8 << 20,
+        flops=10**9,
+        traffic=5 << 20,
         limit=16,
         outs=[pl.BlockSpec(memory_space=pltpu.HBM), VMEM, VMEM],
     )(core_id, edge_source.reshape(groups, 1, GROUP * slots), edge_mult.reshape(groups, 1, GROUP * slots))
@@ -292,7 +295,7 @@
     inv = inv.reshape(per_dev, 128)
 
     here = (blk // 2).astype(jnp.int32).reshape(1)
-    requested = pieces[:, 16, 0].astype(jnp.int32)
+    requested = pieces[:, 32, 0].astype(jnp.int32)
     outgoing, piece = call(
         pick_body,
         [shape((n_blk, BR, width), BF), shape((16, width), BF)],
@@ -306,20 +309,29 @@
     acc = call(
         first_body, shape((per_dev, width), F32), [VMEM] * 3 + [ANY], flops=10**9, traffic=6 << 20, limit=20
     )(main, features, incoming, to_blk)
-    hub_mine = call(copy_body, shape((hubs * HALF, width), BF), [VMEM, VMEM])(
-        exchange(to_blk, "blk").reshape(-1, width), acc
-    )
-    hub_other = swap(hub_mine)
+    hub_mine = exchange(to_blk, "blk").reshape(-1, width)
+    to_swap, acc = lax.optimization_barrier((hub_mine, acc))
+    hub_other = swap(to_swap)
+    acc, hub_cols = call(
+        mid_body,
+        [shape((per_dev, width), F32), shape(dense_hub.shape, BF)],
+        [VMEM] * 3,
+        flops=10**9,
+        traffic=3 << 20,
+        limit=12,
+    )(dense_hub, hub_mine, acc)
 
     output, scaled, keep, send = call(
         layer_body,
-        [shape((per_dev, width), BF)] * 2 + [shape((n_blk, CHUNK, width), BF)] * 2,
-        [SMEM] + [VMEM] * 7,
-        scratch=[pltpu.VMEM((per_dev, width), BF)] * 2 + [pltpu.VMEM((width, width), F32)],
+        [shape((per_dev, width), BF)] * 2 + [shape((n_blk, CHUNK, 128), BF)] * 2,
+        [SMEM] + [VMEM] * 6,
+        scratch=[pltpu.VMEM((per_dev, width), BF)] * 3
+        + [pltpu.VMEM((width, width), F32), pltpu.SemaphoreType.DMA],
+        outs=[VMEM, pl.BlockSpec(memory_space=pltpu.HBM), VMEM, VMEM],
         flops=10**9,
         traffic=6 << 20,
         limit=20,
-    )(core_id, acc, dense_hub, inv, hub_mine, hub_other, weight, cotangent)
+    )(core_id, acc, hub_cols, inv, hub_other, weight, cotangent)
     local_grad, remote_grad = call(
         table_body,
         [shape((per_dev, width), F32), shape((n_blk * BR, width), BF)],
@@ -329,17 +341,11 @@
         limit=20,
     )(main, scaled)
 
-    chunk = shape((CHUNK, width), BF)
-    chunks = shape((n_blk, CHUNK, width), BF)
+    chunk = shape((CHUNK, 128), BF)
+    chunks = shape((n_blk, CHUNK, 128), BF)
     by_blk = exchange(call(pair_body, chunks, [VMEM, VMEM])(keep, swap(send)), "blk")
     part_sum = call(sum_body, chunk, [VMEM])(by_blk)
-    remote_grad = pl.pallas_call(
-        alias_body,
-        out_shape=shape(remote_grad.shape, BF),
-        in_specs=[ANY, VMEM],
-        out_specs=ANY,
-        input_output_aliases={0: 0},
-    )(remote_grad, part_sum)
+    remote_grad, part_sum = lax.optimization_barrier((remote_grad, part_sum))
     returned = exchange(remote_grad.reshape(n_blk, BR, width), "blk")
     full_sum = call(sum_body, chunks, [VMEM, ANY])(lax.all_gather(part_sum, "z"), returned)
     mine = exchange(full_sum, "blk")

time: 189 us -> 181 us (0.958)
  waiting for transfers between devices: 34.2 us -> 30.1 us
    all_to_all x1, waiting for transfers between devices: 6.27 us -> 4.11 us  [shards(): pieces = exchange(offered, 'blk')]
    unnamed x32 -> x26, local copies, waits for them, and re-layouts: 11.3 us -> 10.5 us
  transfers between devices with their start and end apart: 9 -> 9, of which waited for: 8 -> 8; matrix products, arithmetic and copies ran while one was open for 1% -> 2% of each run, Pallas kernels for 4% -> 4%
where the time goes in v3:
time: 181 us; the launch traced here: 180 us
  blocking collectives  62.8 us (35%)
  starting transfers between devices  55.4 us (31%)
  waiting for transfers between devices  30.1 us (17%)
  Pallas kernels  17.2 us (10%)
  local copies, waits for them, and re-layouts  11.8 us (7%)
    all_gather x1, blocking collectives, shards(): along = lax.all_gather(piece, 'z')  25.6 us
    all_gather x1, blocking collectives, shards(): lax.all_gather(part_sum, 'z')  20 us
    all_to_all x1, blocking collectives, shards(): mine = exchange(full_sum, 'blk')  17.3 us
    ppermute x1, starting transfers between devices, shards(): swap(lax.dynamic_index_in_dim(own_halves, 1 - core, 1, keepdims=False))  12.4 us
    unnamed x26, local copies, waits for them, and re-layouts  10.5 us
    all_to_all x1, waiting for transfers between devices, shards(): exchange(call(pair_body, chunks, [VMEM, VMEM])(keep, swap(send)), 'blk')  10.4 us
    ppermute x1, starting transfers between devices, shards(): hub_other = swap(to_swap)  8.82 us
    all_to_all x1, starting transfers between devices, shards(): hub_mine = exchange(to_blk, 'blk').reshape(-1, width)  8.56 us
  transfers between devices with their start and end apart: 9, of which 8 were waited for; matrix products, arithmetic and copies ran while one was open for 2% of the time, Pallas kernels for 4%

profile of v3, /device:TPU:1, one launch (start us, length us, event | category | flops | bytes accessed | tf_op | source)
XLA Modules:
  0.0 179.8 jit_solution(12343791857815522176)
XLA Ops:
  0.6 1.0 dynamic-slice_bitcast_fusion
  1.6 12.4 %collective-permute-start = (bf16[8,32,256]{2,1,0:T(8,128)(2,1)S(1)}, bf16[8,32,256]{2,1,0:T(8,128)(2,1)S(1)}, u32[]{:S(2)}, u32[]{:S(2)}) collective-permute-start(bf16[8,32,256]{2,1,0:T(8,128)(2,1)S(1)} %get-tuple-element.44), channel_id=1, source_target_pairs={{0,1},{1,0},{2,3},{3,2},{4,5},{5,4},{6,7},{7,6},{8,9},{9,8},{10,11... | collective-permute-start | bytes 393224 | tf_op jit(solution)/shard_map/ppermute | solution.py:268
  14.1 0.7 compare_select_fusion
  14.8 0.3 collective-permute-done.got_ref
  15.0 0.7 copy-done.5
  15.7 1.3 shard_map.95
  17.0 3.9 %all-to-all-start = ((bf16[32,40,128]{2,1,0:T(8,128)(2,1)}), bf16[32,40,128]{2,1,0:T(8,128)(2,1)S(1)}, u32[]{:S(2)}, u32[]{:S(2)}) async-start(bf16[32,40,128]{2,1,0:T(8,128)(2,1)} %shard_map.95), calls=%async_computation | async-start | bytes 655360 | tf_op jit(solution)/shard_map/all_to_all | solution.py:273
  20.9 0.9 copy.14
  21.9 0.2 reshape.67.idx_ref
  22.0 0.9 copy.15
  22.9 0.2 reshape.68.mult_ref
  23.1 4.3 %shard_map.94 = (bf16[32,16,2560]{2,1,0:T(8,128)(2,1)S(1)}, bf16[32,16,1024]{2,1,0:T(8,128)(2,1)S(1)}, f32[32,16,128]{2,1,0:T(8,128)S(1)}) custom-call(s32[1]{0:T(128)} %bitcast.core_ref, s32[32,1,256]{2,1,0:T(1,128)S(1)} %reshape.67.idx_ref, s32[32,1,256]{2,1,0:T(1,128)S(1)} %reshape.68.mult_ref), custom_call_target="tpu_custom_call" | custom-call | flops 1000000000 | bytes 5242880 | tf_op jit(solution)/shard_map/pallas_call | solution.py:279
  27.4 1.5 copy-done
  28.9 1.0 copy-done.8
  29.9 4.1 %all-to-all-done.pieces_ref = bf16[32,40,128]{2,1,0:T(8,128)(2,1)S(1)} async-done(((bf16[32,40,128]{2,1,0:T(8,128)(2,1)}), bf16[32,40,128]{2,1,0:T(8,128)(2,1)S(1)}, u32[]{:S(2)}, u32[]{:S(2)}) %all-to-all-start) | async-done | bytes 327712 | tf_op jit(solution)/shard_map/all_to_all | solution.py:273
  34.0 0.7 fusion.which_ref.req_ref
  34.6 1.6 shard_map.96
  36.2 5.1 %all-to-all-start.1 = ((bf16[32,64,256]{2,1,0:T(8,128)(2,1)}), bf16[32,64,256]{2,1,0:T(8,128)(2,1)S(1)}, u32[]{:S(2)}, u32[]{:S(2)}) async-start(bf16[32,64,256]{2,1,0:T(8,128)(2,1)} %get-tuple-element.25), calls=%async_computation.1 | async-start | bytes 2097152 | tf_op jit(solution)/shard_map/all_to_all | solution.py:304
  41.4 25.6 %all-gather = bf16[192,256]{1,0:T(8,128)(2,1)S(1)} all-gather(bf16[16,256]{1,0:T(8,128)(2,1)S(1)} %get-tuple-element.24), channel_id=2, replica_groups=mesh['blk'=32,'z'=12,'core'=2] {'z'}, dimensions={0}, use_global_device_ids=true | all-gather | bytes 106496 | tf_op jit(solution)/shard_map/all_gather | solution.py:305
  66.9 0.6 all-to-all-done.1
  67.6 1.3 shard_map.97._
  68.8 8.6 %all-to-all-start.2 = ((bf16[32,16,256]{2,1,0:T(8,128)(2,1)}), bf16[32,16,256]{2,1,0:T(8,128)(2,1)S(1)}, u32[]{:S(2)}, u32[]{:S(2)}) async-start(bf16[32,16,256]{2,1,0:T(8,128)(2,1)} %shard_map.97._), calls=%async_computation.2 | async-start | bytes 524288 | tf_op jit(solution)/shard_map/all_to_all | solution.py:312
  77.4 1.7 copy-done.1
  79.1 1.4 shard_map.98.acc_ref
  80.5 7.3 %all-to-all-done.2 = bf16[32,16,256]{2,1,0:T(8,128)(2,1)S(1)} async-done(((bf16[32,16,256]{2,1,0:T(8,128)(2,1)}), bf16[32,16,256]{2,1,0:T(8,128)(2,1)S(1)}, u32[]{:S(2)}, u32[]{:S(2)}) %all-to-all-start.2) | async-done | bytes 262176 | tf_op jit(solution)/shard_map/all_to_all | solution.py:312
  87.8 8.8 %collective-permute-start.1 = (bf16[512,256]{1,0:T(8,128)(2,1)S(1)}, bf16[512,256]{1,0:T(8,128)(2,1)S(1)}, u32[]{:S(2)}, u32[]{:S(2)}) collective-permute-start(bf16[512,256]{1,0:T(8,128)(2,1)S(1)} %bitcast.35), channel_id=1, source_target_pairs={{0,1},{1,0},{2,3},{3,2},{4,5},{5,4},{6,7},{7,6},{8,9},{9,8},{10,11... | collective-permute-start | bytes 786440 | tf_op jit(solution)/shard_map/ppermute | solution.py:314
  96.6 1.2 copy-done.9
  97.8 0.5 shard_map.99
  98.4 2.6 %shard_map.100 = (bf16[512,256]{1,0:T(8,128)(2,1)}, bf16[512,256]{1,0:T(8,128)(2,1)S(1)}, bf16[32,40,128]{2,1,0:T(8,128)(2,1)S(1)}, bf16[32,40,128]{2,1,0:T(8,128)(2,1)S(1)}) custom-call(s32[1]{0:T(128)} %bitcast.core_ref, f32[512,256]{1,0:T(8,128)S(1)} %get-tuple-element.28.acc_ref, bf16[512,1024]{1,0:T(8,128)(2,1)S(1)} %get-tuple-element.29.m_ref, ...), custom_call_target="tpu_custom_call" | custom-call | flops 1000000000 | bytes 6291456 | tf_op jit(solution)/shard_map/pallas_call | solution.py:324
  101.0 0.7 copy-done.10
  101.7 1.9 %collective-permute-start.2 = (bf16[32,40,128]{2,1,0:T(8,128)(2,1)S(1)}, bf16[32,40,128]{2,1,0:T(8,128)(2,1)S(1)}, u32[]{:S(2)}, u32[]{:S(2)}) collective-permute-start(bf16[32,40,128]{2,1,0:T(8,128)(2,1)S(1)} %get-tuple-element.36), channel_id=1, source_target_pairs={{0,1},{1,0},{2,3},{3,2},{4,5},{5,4},{6,7},{7,6},{8,9},{9,8},{10,11... | collective-permute-start | bytes 983048 | tf_op jit(solution)/shard_map/ppermute | solution.py:346
  103.6 1.6 collective-permute-done.2.got_ref
  105.2 0.8 shard_map.102
  106.0 3.9 %all-to-all-start.3 = ((bf16[32,40,128]{2,1,0:T(8,128)(2,1)}), bf16[32,40,128]{2,1,0:T(8,128)(2,1)S(1)}, u32[]{:S(2)}, u32[]{:S(2)}) async-start(bf16[32,40,128]{2,1,0:T(8,128)(2,1)} %shard_map.102), calls=%async_computation.3 | async-start | bytes 655360 | tf_op jit(solution)/shard_map/all_to_all | solution.py:346
  109.9 0.9 copy-done.11
  110.8 0.9 shard_map.101
  111.7 1.0 copy-done.4
  112.7 10.4 %all-to-all-done.3.in_ref = bf16[32,40,128]{2,1,0:T(8,128)(2,1)S(1)} async-done(((bf16[32,40,128]{2,1,0:T(8,128)(2,1)}), bf16[32,40,128]{2,1,0:T(8,128)(2,1)S(1)}, u32[]{:S(2)}, u32[]{:S(2)}) %all-to-all-start.3) | async-done | bytes 327712 | tf_op jit(solution)/shard_map/all_to_all | solution.py:346
  123.1 0.1 shard_map.103
  123.2 4.4 %all-to-all-start.4 = ((bf16[32,64,256]{2,1,0:T(8,128)(2,1)}), bf16[32,64,256]{2,1,0:T(8,128)(2,1)S(1)}, u32[]{:S(2)}, u32[]{:S(2)}) async-start(bf16[32,64,256]{2,1,0:T(8,128)(2,1)} %bitcast.29), calls=%async_computation.4 | async-start | bytes 2097152 | tf_op jit(solution)/shard_map/all_to_all | solution.py:349
  127.5 20.0 %all-gather.1 = bf16[480,128]{1,0:T(8,128)(2,1)S(1)} all-gather(bf16[40,128]{1,0:T(8,128)(2,1)S(1)} %shard_map.103), channel_id=3, replica_groups=mesh['blk'=32,'z'=12,'core'=2] {'z'}, dimensions={0}, use_global_device_ids=true | all-gather | bytes 133120 | tf_op jit(solution)/shard_map/all_gather | solution.py:350
  147.5 5.6 %all-to-all-done.4.back_ref.refs_0_ = bf16[32,64,256]{2,1,0:T(8,128)(2,1)S(1)} async-done(((bf16[32,64,256]{2,1,0:T(8,128)(2,1)}), bf16[32,64,256]{2,1,0:T(8,128)(2,1)S(1)}, u32[]{:S(2)}, u32[]{:S(2)}) %all-to-all-start.4) | async-done | bytes 1048608 | tf_op jit(solution)/shard_map/all_to_all | solution.py:349
  153.2 17.3 %all_to_all.30.mine_ref = bf16[32,40,128]{2,1,0:T(8,128)(2,1)S(1)} all-to-all(bf16[32,40,128]{2,1,0:T(8,128)(2,1)S(1)} %shard_map.105), channel_id=1, replica_groups=mesh['blk'=32,'z'=12,'core'=2] {'blk'}, dimensions={0} | all-to-all | bytes 655360 | tf_op jit(solution)/shard_map/all_to_all | solution.py:351
  170.5 6.4 %collective-permute-start.3 = (bf16[32,40,128]{2,1,0:T(8,128)(2,1)S(1)}, bf16[32,40,128]{2,1,0:T(8,128)(2,1)S(1)}, u32[]{:S(2)}, u32[]{:S(2)}) collective-permute-start(bf16[32,40,128]{2,1,0:T(8,128)(2,1)S(1)} %all_to_all.30.mine_ref), channel_id=1, source_target_pairs={{0,1},{1,0},{2,3},{3,2},{4,5},{5,4},{6,7},{7,6},{8,9},{9,8},{10,11... | collective-permute-start | bytes 983048 | tf_op jit(solution)/shard_map/ppermute | solution.py:352
  176.9 0.1 pad_add_fusion.meta_ref
  177.0 0.9 shard_map.104.acc_ref
  177.9 0.3 collective-permute-done.3.other_ref
  178.2 1.6 shard_map.106
  (19 shorter events, 0.1 us)
Async XLA Ops:
  1.6 13.4 %collective-permute-start = (bf16[8,32,256]{2,1,0:T(8,128)(2,1)S(1)}, bf16[8,32,256]{2,1,0:T(8,128)(2,1)S(1)}, u32[]{:S(2)}, u32[]{:S(2)}) collective-permute-start(bf16[8,32,256]{2,1,0:T(8,128)(2,1)S(1)} %get-tuple-element.44), channel_id=1, source_target_pairs={{0,1},{1,0},{2,3},{3,2},{4,5},{5,4},{6,7},{7,6},{8,9},{9,8},{10,11... | collective-permute-start | bytes 393224 | tf_op jit(solution)/shard_map/ppermute | solution.py:268
  15.0 0.7 copy-start.5
  17.0 16.9 %all-to-all-start = ((bf16[32,40,128]{2,1,0:T(8,128)(2,1)}), bf16[32,40,128]{2,1,0:T(8,128)(2,1)S(1)}, u32[]{:S(2)}, u32[]{:S(2)}) async-start(bf16[32,40,128]{2,1,0:T(8,128)(2,1)} %shard_map.95), calls=%async_computation | async-start | bytes 655360 | tf_op jit(solution)/shard_map/all_to_all | solution.py:273
  20.9 13.7 %copy-start.3 = (bf16[512,256]{1,0:T(8,128)(2,1)S(1)}, bf16[512,256]{1,0:T(8,128)(2,1)}, u32[]{:S(2)}) copy-start(bf16[512,256]{1,0:T(8,128)(2,1)} %feat_ref.1) | copy-start | bytes 786436
  27.4 1.5 copy-start
  28.9 1.0 copy-start.8
  36.2 31.3 %all-to-all-start.1 = ((bf16[32,64,256]{2,1,0:T(8,128)(2,1)}), bf16[32,64,256]{2,1,0:T(8,128)(2,1)S(1)}, u32[]{:S(2)}, u32[]{:S(2)}) async-start(bf16[32,64,256]{2,1,0:T(8,128)(2,1)} %get-tuple-element.25), calls=%async_computation.1 | async-start | bytes 2097152 | tf_op jit(solution)/shard_map/all_to_all | solution.py:304
  68.8 19.0 %all-to-all-start.2 = ((bf16[32,16,256]{2,1,0:T(8,128)(2,1)}), bf16[32,16,256]{2,1,0:T(8,128)(2,1)S(1)}, u32[]{:S(2)}, u32[]{:S(2)}) async-start(bf16[32,16,256]{2,1,0:T(8,128)(2,1)} %shard_map.97._), calls=%async_computation.2 | async-start | bytes 524288 | tf_op jit(solution)/shard_map/all_to_all | solution.py:312
  77.4 1.7 copy-start.1
  80.5 17.9 %copy-start.6 = (bf16[512,256]{1,0:T(8,128)(2,1)S(1)}, bf16[512,256]{1,0:T(8,128)(2,1)}, u32[]{:S(2)}) copy-start(bf16[512,256]{1,0:T(8,128)(2,1)} %cot_ref.1) | copy-start | bytes 786436
  80.5 17.9 %copy-start.7 = (bf16[256,256]{1,0:T(8,128)(2,1)S(1)}, bf16[256,256]{1,0:T(8,128)(2,1)}, u32[]{:S(2)}) copy-start(bf16[256,256]{1,0:T(8,128)(2,1)} %weight_ref.1) | copy-start | bytes 393220
  87.8 10.6 %collective-permute-start.1 = (bf16[512,256]{1,0:T(8,128)(2,1)S(1)}, bf16[512,256]{1,0:T(8,128)(2,1)S(1)}, u32[]{:S(2)}, u32[]{:S(2)}) collective-permute-start(bf16[512,256]{1,0:T(8,128)(2,1)S(1)} %bitcast.35), channel_id=1, source_target_pairs={{0,1},{1,0},{2,3},{3,2},{4,5},{5,4},{6,7},{7,6},{8,9},{9,8},{10,11... | collective-permute-start | bytes 786440 | tf_op jit(solution)/shard_map/ppermute | solution.py:314
  96.6 1.2 copy-start.9
  98.4 11.5 %copy-start.2 = (bf16[32,16,2560]{2,1,0:T(8,128)(2,1)S(1)}, bf16[32,16,2560]{2,1,0:T(8,128)(2,1)}, u32[]{:S(2)}) copy-start(bf16[32,16,2560]{2,1,0:T(8,128)(2,1)} %copy-done) | copy-start | bytes 7864324
  101.0 0.7 copy-start.10
  101.7 3.5 %collective-permute-start.2 = (bf16[32,40,128]{2,1,0:T(8,128)(2,1)S(1)}, bf16[32,40,128]{2,1,0:T(8,128)(2,1)S(1)}, u32[]{:S(2)}, u32[]{:S(2)}) collective-permute-start(bf16[32,40,128]{2,1,0:T(8,128)(2,1)S(1)} %get-tuple-element.36), channel_id=1, source_target_pairs={{0,1},{1,0},{2,3},{3,2},{4,5},{5,4},{6,7},{7,6},{8,9},{9,8},{10,11... | collective-permute-start | bytes 983048 | tf_op jit(solution)/shard_map/ppermute | solution.py:346
  106.0 17.1 %all-to-all-start.3 = ((bf16[32,40,128]{2,1,0:T(8,128)(2,1)}), bf16[32,40,128]{2,1,0:T(8,128)(2,1)S(1)}, u32[]{:S(2)}, u32[]{:S(2)}) async-start(bf16[32,40,128]{2,1,0:T(8,128)(2,1)} %shard_map.102), calls=%async_computation.3 | async-start | bytes 655360 | tf_op jit(solution)/shard_map/all_to_all | solution.py:346
  109.9 1.0 copy-start.11
  111.7 1.0 copy-start.4
  123.2 30.0 %all-to-all-start.4 = ((bf16[32,64,256]{2,1,0:T(8,128)(2,1)}), bf16[32,64,256]{2,1,0:T(8,128)(2,1)S(1)}, u32[]{:S(2)}, u32[]{:S(2)}) async-start(bf16[32,64,256]{2,1,0:T(8,128)(2,1)} %bitcast.29), calls=%async_computation.4 | async-start | bytes 2097152 | tf_op jit(solution)/shard_map/all_to_all | solution.py:349
  170.5 7.7 %collective-permute-start.3 = (bf16[32,40,128]{2,1,0:T(8,128)(2,1)S(1)}, bf16[32,40,128]{2,1,0:T(8,128)(2,1)S(1)}, u32[]{:S(2)}, u32[]{:S(2)}) collective-permute-start(bf16[32,40,128]{2,1,0:T(8,128)(2,1)S(1)} %all_to_all.30.mine_ref), channel_id=1, source_target_pairs={{0,1},{1,0},{2,3},{3,2},{4,5},{5,4},{6,7},{7,6},{8,9},{9,8},{10,11... | collective-permute-start | bytes 983048 | tf_op jit(solution)/shard_map/ppermute | solution.py:352

commit v4 on v3

--- a/solution.py
+++ b/solution.py
@@ -97,7 +97,7 @@
         for j in range(2):
             p = 2 * h + j
             put_rows(out_ref, p, block[j * 16 : j * 16 + 16])
-            out_ref[p, 32:40, :] = jnp.full((8, 128), wanted_ref[p].astype(F32), F32).astype(BF)
+            out_ref[p, 32:40, :] = wanted_ref[p]
 
 
 def pick_body(which_ref, here_ref, hub_blk_ref, blocks_ref, pieces_ref, _, out_ref, piece_ref):
@@ -261,14 +261,14 @@
     device = (blk * n_z + z) * 2 + core
 
     own_blocks = features.reshape(blocks_dev, BR, width)
-    wanted = read_blocks.reshape(-1)
+    wanted = jnp.broadcast_to(read_blocks.reshape(n_blk, 1, 1).astype(BF), (n_blk, 8, 128))
 
     own_halves = own_blocks.reshape(blocks_dev, 2, HALF, width)
     kept = lax.dynamic_index_in_dim(own_halves, core, 1, keepdims=False)
     got = swap(lax.dynamic_index_in_dim(own_halves, 1 - core, 1, keepdims=False))
     where_half = (hub_core ^ core) * blocks_dev + hub_local
     offered = call(
-        offer_body, shape((n_blk, CHUNK, 128), BF), [SMEM, SMEM, VMEM, VMEM]
+        offer_body, shape((n_blk, CHUNK, 128), BF), [SMEM, VMEM, VMEM, VMEM]
     )(where_half, wanted, kept, got)
     pieces = exchange(offered, "blk")
 
@@ -343,7 +343,8 @@
 
     chunk = shape((CHUNK, 128), BF)
     chunks = shape((n_blk, CHUNK, 128), BF)
-    by_blk = exchange(call(pair_body, chunks, [VMEM, VMEM])(keep, swap(send)), "blk")
+    got, local_grad, remote_grad = lax.optimization_barrier((swap(send), local_grad, remote_grad))
+    by_blk = exchange(call(pair_body, chunks, [VMEM, VMEM])(keep, got), "blk")
     part_sum = call(sum_body, chunk, [VMEM])(by_blk)
     remote_grad, part_sum = lax.optimization_barrier((remote_grad, part_sum))
     returned = exchange(remote_grad.reshape(n_blk, BR, width), "blk")

time: 181 us -> 178 us (0.983)
  blocking collectives: 62.8 us -> 78.2 us
  waiting for transfers between devices: 30.1 us -> 20.4 us
  local copies, waits for them, and re-layouts: 11.8 us -> 6.46 us
  starting transfers between devices: 55.4 us -> 51.9 us
    all_to_all x0 -> x1, blocking collectives: none -> 16.3 us  [shards(): by_blk = exchange(call(pair_body, chunks, [VMEM, VMEM])(keep, got), 'blk')]
    all_to_all x1 -> x0, waiting for transfers between devices: 10.4 us -> none  [shards(): exchange(call(pair_body, chunks, [VMEM, VMEM])(keep, swap(send)), 'blk')]
    unnamed x26 -> x14, local copies, waits for them, and re-layouts: 10.5 us -> 5.06 us
    all_to_all x1 -> x0, starting transfers between devices: 3.87 us -> none  [shards(): exchange(call(pair_body, chunks, [VMEM, VMEM])(keep, swap(send)), 'blk')]
  transfers between devices with their start and end apart: 9 -> 8, of which waited for: 8 -> 6; matrix products, arithmetic and copies ran while one was open for 2% -> 2% of each run, Pallas kernels for 4% -> 5%
where the time goes in v4:
time: 178 us; the launch traced here: 177 us
  blocking collectives  78.2 us (44%)
  starting transfers between devices  51.9 us (29%)
  waiting for transfers between devices  20.4 us (11%)
  Pallas kernels  17.5 us (10%)
  local copies, waits for them, and re-layouts  6.46 us (4%)
  other arithmetic  2.09 us (1%)
    all_gather x1, blocking collectives, shards(): along = lax.all_gather(piece, 'z')  25.3 us
    all_gather x1, blocking collectives, shards(): lax.all_gather(part_sum, 'z')  19.3 us
    all_to_all x1, blocking collectives, shards(): mine = exchange(full_sum, 'blk')  17.3 us
    all_to_all x1, blocking collectives, shards(): by_blk = exchange(call(pair_body, chunks, [VMEM, VMEM])(keep, got), 'blk')  16.3 us
    ppermute x1, starting transfers between devices, shards(): swap(lax.dynamic_index_in_dim(own_halves, 1 - core, 1, keepdims=False))  12.4 us
    ppermute x1, starting transfers between devices, shards(): hub_other = swap(to_swap)  9.51 us
    all_to_all x1, starting transfers between devices, shards(): hub_mine = exchange(to_blk, 'blk').reshape(-1, width)  8.36 us
    all_to_all x1, waiting for transfers between devices, shards(): hub_mine = exchange(to_blk, 'blk').reshape(-1, width)  7.25 us
  transfers between devices with their start and end apart: 8, of which 6 were waited for; matrix products, arithmetic and copies ran while one was open for 2% of the time, Pallas kernels for 5%

profile of v4, /device:TPU:1, one launch (start us, length us, event | category | flops | bytes accessed | tf_op | source)
XLA Modules:
  0.0 177.5 jit_solution(17243431850439798417)
XLA Ops:
  0.6 1.0 dynamic-slice_bitcast_fusion
  1.6 12.4 %collective-permute-start = (bf16[8,32,256]{2,1,0:T(8,128)(2,1)S(1)}, bf16[8,32,256]{2,1,0:T(8,128)(2,1)S(1)}, u32[]{:S(2)}, u32[]{:S(2)}) collective-permute-start(bf16[8,32,256]{2,1,0:T(8,128)(2,1)S(1)} %get-tuple-element.50), channel_id=1, source_target_pairs={{0,1},{1,0},{2,3},{3,2},{4,5},{5,4},{6,7},{7,6},{8,9},{9,8},{10,11... | collective-permute-start | bytes 393224 | tf_op jit(solution)/shard_map/ppermute | solution.py:268
  14.1 0.7 compare_select_fusion
  14.8 0.7 convert_bitcast_fusion
  15.4 0.0 collective-permute-done.got_ref
  15.4 0.1 broadcast_in_dim.3.wanted_ref
  15.5 1.3 shard_map.95
  16.9 3.9 %all-to-all-start = ((bf16[32,40,128]{2,1,0:T(8,128)(2,1)}), bf16[32,40,128]{2,1,0:T(8,128)(2,1)S(1)}, u32[]{:S(2)}, u32[]{:S(2)}) async-start(bf16[32,40,128]{2,1,0:T(8,128)(2,1)} %shard_map.95), calls=%async_computation | async-start | bytes 655360 | tf_op jit(solution)/shard_map/all_to_all | solution.py:273
  20.8 0.0 copy-start.3
  20.8 0.9 copy.14
  21.7 0.2 reshape.72.idx_ref
  21.9 0.9 copy.15
  22.8 0.2 reshape.73.mult_ref
  22.9 4.3 %shard_map.94 = (bf16[32,16,2560]{2,1,0:T(8,128)(2,1)S(1)}, bf16[32,16,1024]{2,1,0:T(8,128)(2,1)S(1)}, f32[32,16,128]{2,1,0:T(8,128)S(1)}) custom-call(s32[1]{0:T(128)} %bitcast.core_ref, s32[32,1,256]{2,1,0:T(1,128)S(1)} %reshape.72.idx_ref, s32[32,1,256]{2,1,0:T(1,128)S(1)} %reshape.73.mult_ref), custom_call_target="tpu_custom_call" | custom-call | flops 1000000000 | bytes 5242880 | tf_op jit(solution)/shard_map/pallas_call | solution.py:279
  27.2 1.5 copy-done
  28.7 5.3 %all-to-all-done.pieces_ref = bf16[32,40,128]{2,1,0:T(8,128)(2,1)S(1)} async-done(((bf16[32,40,128]{2,1,0:T(8,128)(2,1)}), bf16[32,40,128]{2,1,0:T(8,128)(2,1)S(1)}, u32[]{:S(2)}, u32[]{:S(2)}) %all-to-all-start) | async-done | bytes 327712 | tf_op jit(solution)/shard_map/all_to_all | solution.py:273
  34.1 0.7 fusion.which_ref.req_ref
  34.7 1.6 shard_map.96
  36.3 4.5 %all-to-all-start.1 = ((bf16[32,64,256]{2,1,0:T(8,128)(2,1)}), bf16[32,64,256]{2,1,0:T(8,128)(2,1)S(1)}, u32[]{:S(2)}, u32[]{:S(2)}) async-start(bf16[32,64,256]{2,1,0:T(8,128)(2,1)} %get-tuple-element.28), calls=%async_computation.1 | async-start | bytes 2097152 | tf_op jit(solution)/shard_map/all_to_all | solution.py:304
  40.9 25.3 %all-gather = bf16[192,256]{1,0:T(8,128)(2,1)S(1)} all-gather(bf16[16,256]{1,0:T(8,128)(2,1)S(1)} %get-tuple-element.27), channel_id=2, replica_groups=mesh['blk'=32,'z'=12,'core'=2] {'z'}, dimensions={0}, use_global_device_ids=true | all-gather | bytes 106496 | tf_op jit(solution)/shard_map/all_gather | solution.py:305
  66.1 0.6 all-to-all-done.1
  66.7 1.3 shard_map.97._
  68.0 8.4 %all-to-all-start.2 = ((bf16[32,16,256]{2,1,0:T(8,128)(2,1)}), bf16[32,16,256]{2,1,0:T(8,128)(2,1)S(1)}, u32[]{:S(2)}, u32[]{:S(2)}) async-start(bf16[32,16,256]{2,1,0:T(8,128)(2,1)} %shard_map.97._), calls=%async_computation.2 | async-start | bytes 524288 | tf_op jit(solution)/shard_map/all_to_all | solution.py:312
  76.4 1.7 copy-done.1
  78.1 1.4 shard_map.98.acc_ref
  79.5 0.0 copy-start.4
  79.5 0.0 copy-start.5
  79.5 7.3 %all-to-all-done.2 = bf16[32,16,256]{2,1,0:T(8,128)(2,1)S(1)} async-done(((bf16[32,16,256]{2,1,0:T(8,128)(2,1)}), bf16[32,16,256]{2,1,0:T(8,128)(2,1)S(1)}, u32[]{:S(2)}, u32[]{:S(2)}) %all-to-all-start.2) | async-done | bytes 262176 | tf_op jit(solution)/shard_map/all_to_all | solution.py:312
  86.7 9.5 %collective-permute-start.1 = (bf16[512,256]{1,0:T(8,128)(2,1)S(1)}, bf16[512,256]{1,0:T(8,128)(2,1)S(1)}, u32[]{:S(2)}, u32[]{:S(2)}) collective-permute-start(bf16[512,256]{1,0:T(8,128)(2,1)S(1)} %bitcast.35), channel_id=1, source_target_pairs={{0,1},{1,0},{2,3},{3,2},{4,5},{5,4},{6,7},{7,6},{8,9},{9,8},{10,11... | collective-permute-start | bytes 786440 | tf_op jit(solution)/shard_map/ppermute | solution.py:314
  96.3 0.5 shard_map.99
  96.8 0.6 collective-permute-done.1.other_ref
  97.4 0.0 copy-done.5
  97.4 2.6 %shard_map.100 = (bf16[512,256]{1,0:T(8,128)(2,1)}, bf16[512,256]{1,0:T(8,128)(2,1)S(1)}, bf16[32,40,128]{2,1,0:T(8,128)(2,1)S(1)}, bf16[32,40,128]{2,1,0:T(8,128)(2,1)S(1)}) custom-call(s32[1]{0:T(128)} %bitcast.core_ref, f32[512,256]{1,0:T(8,128)S(1)} %get-tuple-element.31.acc_ref, bf16[512,1024]{1,0:T(8,128)(2,1)S(1)} %get-tuple-element.32.m_ref, ...), custom_call_target="tpu_custom_call" | custom-call | flops 1000000000 | bytes 6291456 | tf_op jit(solution)/shard_map/pallas_call | solution.py:324
  100.0 2.3 %collective-permute-start.2 = (bf16[32,40,128]{2,1,0:T(8,128)(2,1)S(1)}, bf16[32,40,128]{2,1,0:T(8,128)(2,1)S(1)}, u32[]{:S(2)}, u32[]{:S(2)}) collective-permute-start(bf16[32,40,128]{2,1,0:T(8,128)(2,1)S(1)} %get-tuple-element.35), channel_id=1, source_target_pairs={{0,1},{1,0},{2,3},{3,2},{4,5},{5,4},{6,7},{7,6},{8,9},{9,8},{10,11... | collective-permute-start | bytes 983048 | tf_op jit(solution)/shard_map/ppermute | solution.py:346
  102.3 1.9 %shard_map.101 = (f32[512,256]{1,0:T(8,128)S(1)}, bf16[2048,256]{1,0:T(8,128)(2,1)}) custom-call(bf16[512,2560]{1,0:T(8,128)(2,1)S(1)} %bitcast.27, bf16[512,256]{1,0:T(8,128)(2,1)S(1)} %get-tuple-element.36.gs_ref), custom_call_target="tpu_custom_call" | custom-call | flops 1000000000 | bytes 6291456 | tf_op jit(solution)/shard_map/pallas_call | solution.py:335
  104.2 0.0 collective-permute-done.2.got_ref
  104.2 0.1 shard_map.102
  104.3 16.3 %all_to_all.30.in_ref = bf16[32,40,128]{2,1,0:T(8,128)(2,1)S(1)} all-to-all(bf16[32,40,128]{2,1,0:T(8,128)(2,1)S(1)} %shard_map.102), channel_id=1, replica_groups=mesh['blk'=32,'z'=12,'core'=2] {'blk'}, dimensions={0} | all-to-all | bytes 655360 | tf_op jit(solution)/shard_map/all_to_all | solution.py:347
  120.6 0.1 shard_map.103
  120.7 4.6 %all-to-all-start.4 = ((bf16[32,64,256]{2,1,0:T(8,128)(2,1)}), bf16[32,64,256]{2,1,0:T(8,128)(2,1)S(1)}, u32[]{:S(2)}, u32[]{:S(2)}) async-start(bf16[32,64,256]{2,1,0:T(8,128)(2,1)} %bitcast.14), calls=%async_computation.4 | async-start | bytes 2097152 | tf_op jit(solution)/shard_map/all_to_all | solution.py:350
  125.2 19.3 %all-gather.1 = bf16[480,128]{1,0:T(8,128)(2,1)S(1)} all-gather(bf16[40,128]{1,0:T(8,128)(2,1)S(1)} %shard_map.103), channel_id=3, replica_groups=mesh['blk'=32,'z'=12,'core'=2] {'z'}, dimensions={0}, use_global_device_ids=true | all-gather | bytes 133120 | tf_op jit(solution)/shard_map/all_gather | solution.py:351
  144.5 6.4 %all-to-all-done.4.back_ref.refs_0_ = bf16[32,64,256]{2,1,0:T(8,128)(2,1)S(1)} async-done(((bf16[32,64,256]{2,1,0:T(8,128)(2,1)}), bf16[32,64,256]{2,1,0:T(8,128)(2,1)S(1)}, u32[]{:S(2)}, u32[]{:S(2)}) %all-to-all-start.4) | async-done | bytes 1048608 | tf_op jit(solution)/shard_map/all_to_all | solution.py:350
  150.9 17.3 %all_to_all.31.mine_ref = bf16[32,40,128]{2,1,0:T(8,128)(2,1)S(1)} all-to-all(bf16[32,40,128]{2,1,0:T(8,128)(2,1)S(1)} %shard_map.105), channel_id=1, replica_groups=mesh['blk'=32,'z'=12,'core'=2] {'blk'}, dimensions={0} | all-to-all | bytes 655360 | tf_op jit(solution)/shard_map/all_to_all | solution.py:352
  168.2 6.4 %collective-permute-start.3 = (bf16[32,40,128]{2,1,0:T(8,128)(2,1)S(1)}, bf16[32,40,128]{2,1,0:T(8,128)(2,1)S(1)}, u32[]{:S(2)}, u32[]{:S(2)}) collective-permute-start(bf16[32,40,128]{2,1,0:T(8,128)(2,1)S(1)} %all_to_all.31.mine_ref), channel_id=1, source_target_pairs={{0,1},{1,0},{2,3},{3,2},{4,5},{5,4},{6,7},{7,6},{8,9},{9,8},{10,11... | collective-permute-start | bytes 983048 | tf_op jit(solution)/shard_map/ppermute | solution.py:353
  174.6 0.1 pad_add_fusion.meta_ref
  174.7 0.9 shard_map.104.acc_ref
  175.6 0.3 collective-permute-done.3.other_ref
  175.9 1.6 shard_map.106
  (8 shorter events, 0.1 us)
Async XLA Ops:
  1.6 13.8 %collective-permute-start = (bf16[8,32,256]{2,1,0:T(8,128)(2,1)S(1)}, bf16[8,32,256]{2,1,0:T(8,128)(2,1)S(1)}, u32[]{:S(2)}, u32[]{:S(2)}) collective-permute-start(bf16[8,32,256]{2,1,0:T(8,128)(2,1)S(1)} %get-tuple-element.50), channel_id=1, source_target_pairs={{0,1},{1,0},{2,3},{3,2},{4,5},{5,4},{6,7},{7,6},{8,9},{9,8},{10,11... | collective-permute-start | bytes 393224 | tf_op jit(solution)/shard_map/ppermute | solution.py:268
  16.9 17.2 %all-to-all-start = ((bf16[32,40,128]{2,1,0:T(8,128)(2,1)}), bf16[32,40,128]{2,1,0:T(8,128)(2,1)S(1)}, u32[]{:S(2)}, u32[]{:S(2)}) async-start(bf16[32,40,128]{2,1,0:T(8,128)(2,1)} %shard_map.95), calls=%async_computation | async-start | bytes 655360 | tf_op jit(solution)/shard_map/all_to_all | solution.py:273
  20.8 14.0 %copy-start.3 = (bf16[512,256]{1,0:T(8,128)(2,1)S(1)}, bf16[512,256]{1,0:T(8,128)(2,1)}, u32[]{:S(2)}) copy-start(bf16[512,256]{1,0:T(8,128)(2,1)} %feat_ref.1) | copy-start | bytes 786436
  27.2 1.5 copy-start
  36.3 30.4 %all-to-all-start.1 = ((bf16[32,64,256]{2,1,0:T(8,128)(2,1)}), bf16[32,64,256]{2,1,0:T(8,128)(2,1)S(1)}, u32[]{:S(2)}, u32[]{:S(2)}) async-start(bf16[32,64,256]{2,1,0:T(8,128)(2,1)} %get-tuple-element.28), calls=%async_computation.1 | async-start | bytes 2097152 | tf_op jit(solution)/shard_map/all_to_all | solution.py:304
  68.0 18.8 %all-to-all-start.2 = ((bf16[32,16,256]{2,1,0:T(8,128)(2,1)}), bf16[32,16,256]{2,1,0:T(8,128)(2,1)S(1)}, u32[]{:S(2)}, u32[]{:S(2)}) async-start(bf16[32,16,256]{2,1,0:T(8,128)(2,1)} %shard_map.97._), calls=%async_computation.2 | async-start | bytes 524288 | tf_op jit(solution)/shard_map/all_to_all | solution.py:312
  76.3 1.7 copy-start.1
  79.5 17.9 %copy-start.4 = (bf16[512,256]{1,0:T(8,128)(2,1)S(1)}, bf16[512,256]{1,0:T(8,128)(2,1)}, u32[]{:S(2)}) copy-start(bf16[512,256]{1,0:T(8,128)(2,1)} %cot_ref.1) | copy-start | bytes 786436
  79.5 17.9 %copy-start.5 = (bf16[256,256]{1,0:T(8,128)(2,1)S(1)}, bf16[256,256]{1,0:T(8,128)(2,1)}, u32[]{:S(2)}) copy-start(bf16[256,256]{1,0:T(8,128)(2,1)} %weight_ref.1) | copy-start | bytes 393220
  86.7 10.7 %collective-permute-start.1 = (bf16[512,256]{1,0:T(8,128)(2,1)S(1)}, bf16[512,256]{1,0:T(8,128)(2,1)S(1)}, u32[]{:S(2)}, u32[]{:S(2)}) collective-permute-start(bf16[512,256]{1,0:T(8,128)(2,1)S(1)} %bitcast.35), channel_id=1, source_target_pairs={{0,1},{1,0},{2,3},{3,2},{4,5},{5,4},{6,7},{7,6},{8,9},{9,8},{10,11... | collective-permute-start | bytes 786440 | tf_op jit(solution)/shard_map/ppermute | solution.py:314
  96.8 5.5 %copy-start.2 = (bf16[32,16,2560]{2,1,0:T(8,128)(2,1)S(1)}, bf16[32,16,2560]{2,1,0:T(8,128)(2,1)}, u32[]{:S(2)}) copy-start(bf16[32,16,2560]{2,1,0:T(8,128)(2,1)} %copy-done) | copy-start | bytes 7864324
  100.0 4.2 %collective-permute-start.2 = (bf16[32,40,128]{2,1,0:T(8,128)(2,1)S(1)}, bf16[32,40,128]{2,1,0:T(8,128)(2,1)S(1)}, u32[]{:S(2)}, u32[]{:S(2)}) collective-permute-start(bf16[32,40,128]{2,1,0:T(8,128)(2,1)S(1)} %get-tuple-element.35), channel_id=1, source_target_pairs={{0,1},{1,0},{2,3},{3,2},{4,5},{5,4},{6,7},{7,6},{8,9},{9,8},{10,11... | collective-permute-start | bytes 983048 | tf_op jit(solution)/shard_map/ppermute | solution.py:346
  120.7 30.2 %all-to-all-start.4 = ((bf16[32,64,256]{2,1,0:T(8,128)(2,1)}), bf16[32,64,256]{2,1,0:T(8,128)(2,1)S(1)}, u32[]{:S(2)}, u32[]{:S(2)}) async-start(bf16[32,64,256]{2,1,0:T(8,128)(2,1)} %bitcast.14), calls=%async_computation.4 | async-start | bytes 2097152 | tf_op jit(solution)/shard_map/all_to_all | solution.py:350
  168.2 7.6 %collective-permute-start.3 = (bf16[32,40,128]{2,1,0:T(8,128)(2,1)S(1)}, bf16[32,40,128]{2,1,0:T(8,128)(2,1)S(1)}, u32[]{:S(2)}, u32[]{:S(2)}) collective-permute-start(bf16[32,40,128]{2,1,0:T(8,128)(2,1)S(1)} %all_to_all.31.mine_ref), channel_id=1, source_target_pairs={{0,1},{1,0},{2,3},{3,2},{4,5},{5,4},{6,7},{7,6},{8,9},{9,8},{10,11... | collective-permute-start | bytes 983048 | tf_op jit(solution)/shard_map/ppermute | solution.py:353

commit v5 on v4

--- a/solution.py
+++ b/solution.py
@@ -88,12 +88,13 @@
     return jnp.concatenate([ref[at, 0:16, :], ref[at, 16:32, :]], axis=1)
 
 
-def offer_body(which_ref, wanted_ref, kept_ref, got_ref, out_ref):
+def offer_body(core_ref, hub_ref, wanted_ref, kept_ref, got_ref, out_ref):
     rows = kept_ref.shape[0]
     for h in range(out_ref.shape[0] // 2):
-        at = which_ref[h]
-        inner = jnp.where(at < rows, at, at - rows)
-        block = jnp.where(at < rows, kept_ref[inner], got_ref[inner])
+        hub = hub_ref[h]
+        inner = hub & (rows - 1)
+        own = ((hub // rows) & 1) == core_ref[0]
+        block = jnp.where(own, kept_ref[inner], got_ref[inner])
         for j in range(2):
             p = 2 * h + j
             put_rows(out_ref, p, block[j * 16 : j * 16 + 16])
@@ -257,7 +258,6 @@
     hub_local = hub_blocks % blocks_dev
     hub_blk = hub_device // (2 * n_z)
     hub_z = (hub_device // 2) % n_z
-    hub_core = hub_device % 2
     device = (blk * n_z + z) * 2 + core
 
     own_blocks = features.reshape(blocks_dev, BR, width)
@@ -266,14 +266,13 @@
     own_halves = own_blocks.reshape(blocks_dev, 2, HALF, width)
     kept = lax.dynamic_index_in_dim(own_halves, core, 1, keepdims=False)
     got = swap(lax.dynamic_index_in_dim(own_halves, 1 - core, 1, keepdims=False))
-    where_half = (hub_core ^ core) * blocks_dev + hub_local
+    core_id = core.astype(jnp.int32).reshape(1)
     offered = call(
-        offer_body, shape((n_blk, CHUNK, 128), BF), [SMEM, VMEM, VMEM, VMEM]
-    )(where_half, wanted, kept, got)
+        offer_body, shape((n_blk, CHUNK, 128), BF), [SMEM, SMEM, VMEM, VMEM, VMEM]
+    )(core_id, hub_blocks, wanted, kept, got)
     pieces = exchange(offered, "blk")
 
     n_half = hubs * HALF
-    core_id = core.astype(jnp.int32).reshape(1)
     groups = per_dev // GROUP
     main_rows = per_dev + n_blk * BR
     main, dense_hub, inv = call(

time: 178 us -> 179 us (level)
    unnamed x14 -> x18, local copies, waits for them, and re-layouts: 5.06 us -> 5.7 us
  transfers between devices with their start and end apart: 8 -> 8, of which waited for: 6 -> 7; matrix products, arithmetic and copies ran while one was open for 2% -> 2% of each run, Pallas kernels for 5% -> 5%
where the time goes in v5:
time: 179 us; the launch traced here: 178 us
  blocking collectives  78.5 us (44%)
  starting transfers between devices  52.4 us (29%)
  waiting for transfers between devices  19.9 us (11%)
  Pallas kernels  17.6 us (10%)
  local copies, waits for them, and re-layouts  7.1 us (4%)
    all_gather x1, blocking collectives, shards(): along = lax.all_gather(piece, 'z')  25.6 us
    all_gather x1, blocking collectives, shards(): lax.all_gather(part_sum, 'z')  19.3 us
    all_to_all x1, blocking collectives, shards(): mine = exchange(full_sum, 'blk')  17.3 us
    all_to_all x1, blocking collectives, shards(): by_blk = exchange(call(pair_body, chunks, [VMEM, VMEM])(keep, got), 'blk')  16.3 us
    ppermute x1, starting transfers between devices, shards(): swap(lax.dynamic_index_in_dim(own_halves, 1 - core, 1, keepdims=False))  12.4 us
    ppermute x1, starting transfers between devices, shards(): hub_other = swap(to_swap)  9.5 us
    all_to_all x1, starting transfers between devices, shards(): hub_mine = exchange(to_blk, 'blk').reshape(-1, width)  8.91 us
    all_to_all x1, waiting for transfers between devices, shards(): hub_mine = exchange(to_blk, 'blk').reshape(-1, width)  7.25 us
  transfers between devices with their start and end apart: 8, of which 7 were waited for; matrix products, arithmetic and copies ran while one was open for 2% of the time, Pallas kernels for 5%

profile of v5, /device:TPU:1, one launch (start us, length us, event | category | flops | bytes accessed | tf_op | source)
XLA Modules:
  0.0 177.8 jit_solution(18175785409779961940)
XLA Ops:
  0.6 1.0 dynamic-slice_bitcast_fusion
  1.6 12.4 %collective-permute-start = (bf16[8,32,256]{2,1,0:T(8,128)(2,1)S(1)}, bf16[8,32,256]{2,1,0:T(8,128)(2,1)S(1)}, u32[]{:S(2)}, u32[]{:S(2)}) collective-permute-start(bf16[8,32,256]{2,1,0:T(8,128)(2,1)S(1)} %get-tuple-element.49), channel_id=1, source_target_pairs={{0,1},{1,0},{2,3},{3,2},{4,5},{5,4},{6,7},{7,6},{8,9},{9,8},{10,11... | collective-permute-start | bytes 393224 | tf_op jit(solution)/shard_map/ppermute | solution.py:268
  14.1 0.7 convert_bitcast_fusion
  14.7 0.3 collective-permute-done.got_ref
  15.0 0.1 broadcast_in_dim.3.wanted_ref
  15.1 0.0 copy-start.4
  15.1 0.6 copy-done.4
  15.8 1.4 shard_map.95
  17.2 3.9 %all-to-all-start = ((bf16[32,40,128]{2,1,0:T(8,128)(2,1)}), bf16[32,40,128]{2,1,0:T(8,128)(2,1)S(1)}, u32[]{:S(2)}, u32[]{:S(2)}) async-start(bf16[32,40,128]{2,1,0:T(8,128)(2,1)} %shard_map.95), calls=%async_computation | async-start | bytes 655360 | tf_op jit(solution)/shard_map/all_to_all | solution.py:273
  21.1 0.0 copy-start.5
  21.1 0.0 copy-start.3
  21.1 0.9 copy.14
  22.0 0.2 reshape.72.idx_ref
  22.2 0.9 copy.15
  23.1 0.2 reshape.73.mult_ref
  23.3 4.3 %shard_map.94 = (bf16[32,16,2560]{2,1,0:T(8,128)(2,1)S(1)}, bf16[32,16,1024]{2,1,0:T(8,128)(2,1)S(1)}, f32[32,16,128]{2,1,0:T(8,128)S(1)}) custom-call(s32[1]{0:T(128)} %bitcast.core_ref, s32[32,1,256]{2,1,0:T(1,128)S(1)} %reshape.72.idx_ref, s32[32,1,256]{2,1,0:T(1,128)S(1)} %reshape.73.mult_ref), custom_call_target="tpu_custom_call" | custom-call | flops 1000000000 | bytes 5242880 | tf_op jit(solution)/shard_map/pallas_call | solution.py:278
  27.6 1.5 copy-done
  29.1 5.0 %all-to-all-done.pieces_ref = bf16[32,40,128]{2,1,0:T(8,128)(2,1)S(1)} async-done(((bf16[32,40,128]{2,1,0:T(8,128)(2,1)}), bf16[32,40,128]{2,1,0:T(8,128)(2,1)S(1)}, u32[]{:S(2)}, u32[]{:S(2)}) %all-to-all-start) | async-done | bytes 327712 | tf_op jit(solution)/shard_map/all_to_all | solution.py:273
  34.1 0.7 fusion.which_ref.req_ref
  34.8 1.6 shard_map.96
  36.4 4.4 %all-to-all-start.1 = ((bf16[32,64,256]{2,1,0:T(8,128)(2,1)}), bf16[32,64,256]{2,1,0:T(8,128)(2,1)S(1)}, u32[]{:S(2)}, u32[]{:S(2)}) async-start(bf16[32,64,256]{2,1,0:T(8,128)(2,1)} %get-tuple-element.28), calls=%async_computation.1 | async-start | bytes 2097152 | tf_op jit(solution)/shard_map/all_to_all | solution.py:303
  40.8 25.6 %all-gather = bf16[192,256]{1,0:T(8,128)(2,1)S(1)} all-gather(bf16[16,256]{1,0:T(8,128)(2,1)S(1)} %get-tuple-element.27), channel_id=2, replica_groups=mesh['blk'=32,'z'=12,'core'=2] {'z'}, dimensions={0}, use_global_device_ids=true | all-gather | bytes 106496 | tf_op jit(solution)/shard_map/all_gather | solution.py:304
  66.4 0.1 all-to-all-done.1
  66.5 1.3 shard_map.97._
  67.7 8.9 %all-to-all-start.2 = ((bf16[32,16,256]{2,1,0:T(8,128)(2,1)}), bf16[32,16,256]{2,1,0:T(8,128)(2,1)S(1)}, u32[]{:S(2)}, u32[]{:S(2)}) async-start(bf16[32,16,256]{2,1,0:T(8,128)(2,1)} %shard_map.97._), calls=%async_computation.2 | async-start | bytes 524288 | tf_op jit(solution)/shard_map/all_to_all | solution.py:311
  76.6 1.7 copy-done.1
  78.4 1.4 shard_map.98.acc_ref
  79.8 0.0 copy-start.6
  79.8 0.0 copy-start.7
  79.8 7.2 %all-to-all-done.2 = bf16[32,16,256]{2,1,0:T(8,128)(2,1)S(1)} async-done(((bf16[32,16,256]{2,1,0:T(8,128)(2,1)}), bf16[32,16,256]{2,1,0:T(8,128)(2,1)S(1)}, u32[]{:S(2)}, u32[]{:S(2)}) %all-to-all-start.2) | async-done | bytes 262176 | tf_op jit(solution)/shard_map/all_to_all | solution.py:311
  87.0 9.5 %collective-permute-start.1 = (bf16[512,256]{1,0:T(8,128)(2,1)S(1)}, bf16[512,256]{1,0:T(8,128)(2,1)S(1)}, u32[]{:S(2)}, u32[]{:S(2)}) collective-permute-start(bf16[512,256]{1,0:T(8,128)(2,1)S(1)} %bitcast.35), channel_id=1, source_target_pairs={{0,1},{1,0},{2,3},{3,2},{4,5},{5,4},{6,7},{7,6},{8,9},{9,8},{10,11... | collective-permute-start | bytes 786440 | tf_op jit(solution)/shard_map/ppermute | solution.py:313
  96.5 0.5 shard_map.99
  97.1 0.6 collective-permute-done.1.other_ref
  97.7 2.6 %shard_map.100 = (bf16[512,256]{1,0:T(8,128)(2,1)}, bf16[512,256]{1,0:T(8,128)(2,1)S(1)}, bf16[32,40,128]{2,1,0:T(8,128)(2,1)S(1)}, bf16[32,40,128]{2,1,0:T(8,128)(2,1)S(1)}) custom-call(s32[1]{0:T(128)} %bitcast.core_ref, f32[512,256]{1,0:T(8,128)S(1)} %get-tuple-element.31.acc_ref, bf16[512,1024]{1,0:T(8,128)(2,1)S(1)} %get-tuple-element.32.m_ref, ...), custom_call_target="tpu_custom_call" | custom-call | flops 1000000000 | bytes 6291456 | tf_op jit(solution)/shard_map/pallas_call | solution.py:323
  100.3 2.3 %collective-permute-start.2 = (bf16[32,40,128]{2,1,0:T(8,128)(2,1)S(1)}, bf16[32,40,128]{2,1,0:T(8,128)(2,1)S(1)}, u32[]{:S(2)}, u32[]{:S(2)}) collective-permute-start(bf16[32,40,128]{2,1,0:T(8,128)(2,1)S(1)} %get-tuple-element.35), channel_id=1, source_target_pairs={{0,1},{1,0},{2,3},{3,2},{4,5},{5,4},{6,7},{7,6},{8,9},{9,8},{10,11... | collective-permute-start | bytes 983048 | tf_op jit(solution)/shard_map/ppermute | solution.py:345
  102.6 1.9 %shard_map.101 = (f32[512,256]{1,0:T(8,128)S(1)}, bf16[2048,256]{1,0:T(8,128)(2,1)}) custom-call(bf16[512,2560]{1,0:T(8,128)(2,1)S(1)} %bitcast.27, bf16[512,256]{1,0:T(8,128)(2,1)S(1)} %get-tuple-element.36.gs_ref), custom_call_target="tpu_custom_call" | custom-call | flops 1000000000 | bytes 6291456 | tf_op jit(solution)/shard_map/pallas_call | solution.py:334
  104.5 0.1 shard_map.102
  104.6 16.3 %all_to_all.30.in_ref = bf16[32,40,128]{2,1,0:T(8,128)(2,1)S(1)} all-to-all(bf16[32,40,128]{2,1,0:T(8,128)(2,1)S(1)} %shard_map.102), channel_id=1, replica_groups=mesh['blk'=32,'z'=12,'core'=2] {'blk'}, dimensions={0} | all-to-all | bytes 655360 | tf_op jit(solution)/shard_map/all_to_all | solution.py:346
  120.9 0.1 shard_map.103
  121.0 4.5 %all-to-all-start.4 = ((bf16[32,64,256]{2,1,0:T(8,128)(2,1)}), bf16[32,64,256]{2,1,0:T(8,128)(2,1)S(1)}, u32[]{:S(2)}, u32[]{:S(2)}) async-start(bf16[32,64,256]{2,1,0:T(8,128)(2,1)} %bitcast.14), calls=%async_computation.4 | async-start | bytes 2097152 | tf_op jit(solution)/shard_map/all_to_all | solution.py:349
  125.5 19.3 %all-gather.1 = bf16[480,128]{1,0:T(8,128)(2,1)S(1)} all-gather(bf16[40,128]{1,0:T(8,128)(2,1)S(1)} %shard_map.103), channel_id=3, replica_groups=mesh['blk'=32,'z'=12,'core'=2] {'z'}, dimensions={0}, use_global_device_ids=true | all-gather | bytes 133120 | tf_op jit(solution)/shard_map/all_gather | solution.py:350
  144.8 6.4 %all-to-all-done.4.back_ref.refs_0_ = bf16[32,64,256]{2,1,0:T(8,128)(2,1)S(1)} async-done(((bf16[32,64,256]{2,1,0:T(8,128)(2,1)}), bf16[32,64,256]{2,1,0:T(8,128)(2,1)S(1)}, u32[]{:S(2)}, u32[]{:S(2)}) %all-to-all-start.4) | async-done | bytes 1048608 | tf_op jit(solution)/shard_map/all_to_all | solution.py:349
  151.2 17.3 %all_to_all.31.mine_ref = bf16[32,40,128]{2,1,0:T(8,128)(2,1)S(1)} all-to-all(bf16[32,40,128]{2,1,0:T(8,128)(2,1)S(1)} %shard_map.105), channel_id=1, replica_groups=mesh['blk'=32,'z'=12,'core'=2] {'blk'}, dimensions={0} | all-to-all | bytes 655360 | tf_op jit(solution)/shard_map/all_to_all | solution.py:351
  168.5 6.4 %collective-permute-start.3 = (bf16[32,40,128]{2,1,0:T(8,128)(2,1)S(1)}, bf16[32,40,128]{2,1,0:T(8,128)(2,1)S(1)}, u32[]{:S(2)}, u32[]{:S(2)}) collective-permute-start(bf16[32,40,128]{2,1,0:T(8,128)(2,1)S(1)} %all_to_all.31.mine_ref), channel_id=1, source_target_pairs={{0,1},{1,0},{2,3},{3,2},{4,5},{5,4},{6,7},{7,6},{8,9},{9,8},{10,11... | collective-permute-start | bytes 983048 | tf_op jit(solution)/shard_map/ppermute | solution.py:352
  174.9 0.1 pad_add_fusion.meta_ref
  175.0 0.9 shard_map.104.acc_ref
  175.9 0.3 collective-permute-done.3.other_ref
  176.2 1.6 shard_map.106
  (12 shorter events, 0.1 us)
Async XLA Ops:
  1.6 13.4 %collective-permute-start = (bf16[8,32,256]{2,1,0:T(8,128)(2,1)S(1)}, bf16[8,32,256]{2,1,0:T(8,128)(2,1)S(1)}, u32[]{:S(2)}, u32[]{:S(2)}) collective-permute-start(bf16[8,32,256]{2,1,0:T(8,128)(2,1)S(1)} %get-tuple-element.49), channel_id=1, source_target_pairs={{0,1},{1,0},{2,3},{3,2},{4,5},{5,4},{6,7},{7,6},{8,9},{9,8},{10,11... | collective-permute-start | bytes 393224 | tf_op jit(solution)/shard_map/ppermute | solution.py:268
  15.1 0.7 copy-start.4
  17.2 16.9 %all-to-all-start = ((bf16[32,40,128]{2,1,0:T(8,128)(2,1)}), bf16[32,40,128]{2,1,0:T(8,128)(2,1)S(1)}, u32[]{:S(2)}, u32[]{:S(2)}) async-start(bf16[32,40,128]{2,1,0:T(8,128)(2,1)} %shard_map.95), calls=%async_computation | async-start | bytes 655360 | tf_op jit(solution)/shard_map/all_to_all | solution.py:273
  21.1 8.0 %copy-start.5 = (s32[16]{0:T(128)S(1)}, s32[16]{0:T(128)}, u32[]{:S(2)}) copy-start(s32[16]{0:T(128)} %hub_ref.1) | copy-start | bytes 196
  21.1 13.7 %copy-start.3 = (bf16[512,256]{1,0:T(8,128)(2,1)S(1)}, bf16[512,256]{1,0:T(8,128)(2,1)}, u32[]{:S(2)}) copy-start(bf16[512,256]{1,0:T(8,128)(2,1)} %feat_ref.1) | copy-start | bytes 786436
  27.5 1.5 copy-start
  36.4 30.1 %all-to-all-start.1 = ((bf16[32,64,256]{2,1,0:T(8,128)(2,1)}), bf16[32,64,256]{2,1,0:T(8,128)(2,1)S(1)}, u32[]{:S(2)}, u32[]{:S(2)}) async-start(bf16[32,64,256]{2,1,0:T(8,128)(2,1)} %get-tuple-element.28), calls=%async_computation.1 | async-start | bytes 2097152 | tf_op jit(solution)/shard_map/all_to_all | solution.py:303
  67.7 19.3 %all-to-all-start.2 = ((bf16[32,16,256]{2,1,0:T(8,128)(2,1)}), bf16[32,16,256]{2,1,0:T(8,128)(2,1)S(1)}, u32[]{:S(2)}, u32[]{:S(2)}) async-start(bf16[32,16,256]{2,1,0:T(8,128)(2,1)} %shard_map.97._), calls=%async_computation.2 | async-start | bytes 524288 | tf_op jit(solution)/shard_map/all_to_all | solution.py:311
  76.6 1.7 copy-start.1
  79.8 17.9 %copy-start.6 = (bf16[512,256]{1,0:T(8,128)(2,1)S(1)}, bf16[512,256]{1,0:T(8,128)(2,1)}, u32[]{:S(2)}) copy-start(bf16[512,256]{1,0:T(8,128)(2,1)} %cot_ref.1) | copy-start | bytes 786436
  79.8 17.9 %copy-start.7 = (bf16[256,256]{1,0:T(8,128)(2,1)S(1)}, bf16[256,256]{1,0:T(8,128)(2,1)}, u32[]{:S(2)}) copy-start(bf16[256,256]{1,0:T(8,128)(2,1)} %weight_ref.1) | copy-start | bytes 393220
  87.0 10.7 %collective-permute-start.1 = (bf16[512,256]{1,0:T(8,128)(2,1)S(1)}, bf16[512,256]{1,0:T(8,128)(2,1)S(1)}, u32[]{:S(2)}, u32[]{:S(2)}) collective-permute-start(bf16[512,256]{1,0:T(8,128)(2,1)S(1)} %bitcast.35), channel_id=1, source_target_pairs={{0,1},{1,0},{2,3},{3,2},{4,5},{5,4},{6,7},{7,6},{8,9},{9,8},{10,11... | collective-permute-start | bytes 786440 | tf_op jit(solution)/shard_map/ppermute | solution.py:313
  97.1 5.5 %copy-start.2 = (bf16[32,16,2560]{2,1,0:T(8,128)(2,1)S(1)}, bf16[32,16,2560]{2,1,0:T(8,128)(2,1)}, u32[]{:S(2)}) copy-start(bf16[32,16,2560]{2,1,0:T(8,128)(2,1)} %copy-done) | copy-start | bytes 7864324
  100.3 4.2 %collective-permute-start.2 = (bf16[32,40,128]{2,1,0:T(8,128)(2,1)S(1)}, bf16[32,40,128]{2,1,0:T(8,128)(2,1)S(1)}, u32[]{:S(2)}, u32[]{:S(2)}) collective-permute-start(bf16[32,40,128]{2,1,0:T(8,128)(2,1)S(1)} %get-tuple-element.35), channel_id=1, source_target_pairs={{0,1},{1,0},{2,3},{3,2},{4,5},{5,4},{6,7},{7,6},{8,9},{9,8},{10,11... | collective-permute-start | bytes 983048 | tf_op jit(solution)/shard_map/ppermute | solution.py:345
  121.0 30.2 %all-to-all-start.4 = ((bf16[32,64,256]{2,1,0:T(8,128)(2,1)}), bf16[32,64,256]{2,1,0:T(8,128)(2,1)S(1)}, u32[]{:S(2)}, u32[]{:S(2)}) async-start(bf16[32,64,256]{2,1,0:T(8,128)(2,1)} %bitcast.14), calls=%async_computation.4 | async-start | bytes 2097152 | tf_op jit(solution)/shard_map/all_to_all | solution.py:349
  168.5 7.6 %collective-permute-start.3 = (bf16[32,40,128]{2,1,0:T(8,128)(2,1)S(1)}, bf16[32,40,128]{2,1,0:T(8,128)(2,1)S(1)}, u32[]{:S(2)}, u32[]{:S(2)}) collective-permute-start(bf16[32,40,128]{2,1,0:T(8,128)(2,1)S(1)} %all_to_all.31.mine_ref), channel_id=1, source_target_pairs={{0,1},{1,0},{2,3},{3,2},{4,5},{5,4},{6,7},{7,6},{8,9},{9,8},{10,11... | collective-permute-start | bytes 983048 | tf_op jit(solution)/shard_map/ppermute | solution.py:352
